TPU v7x, 256 devices: a whole 4x4x8 slice. The times are simulated.
256 devices in a mesh: seq: 64 (over y_lo, z, x), chan: 4 (over y_hi, core).
Axes of the slice: x: 4, y: 4 (y_hi: 2, y_lo: 2; y = y_hi * 2 + y_lo), z: 8, core: 2. Of those that a mesh axis runs over, the one named last changes fastest.
Arguments:
- features: bfloat16 [16384, 4096], P('seq', 'chan'), may hold values from -6 to 6
- w_in: bfloat16 [4096, 3, 2048], P('seq', None, 'chan'), may hold values from -0.09375 to 0.09375
- filter_real: float32 [16384, 2048], P('seq', 'chan'), may hold values from -6 to 6
- filter_imag: float32 [16384, 2048], P('seq', 'chan'), may hold values from -6 to 6
- skip_gain: float32 [2048], P('chan'), may hold values from -4 to 4
Outputs:
- gated_output: bfloat16 [16384, 2048], P('seq', 'chan')
All inputs are finite; a program needn't handle non-finite values.
Results may differ from a plain program's by a relative error of at most 0.0064.
Values may be sent and summed in bfloat16 or wider, within the bound.
A program may use at most 128 MiB of HBM per device.

v0:
```python
import math

import jax
import jax.numpy as jnp
from jax import lax
from jax.sharding import PartitionSpec as P

TWO_PI = 2.0 * math.pi
HIGHEST = lax.Precision.HIGHEST


def swapped(block, axis, distance):
    count = lax.axis_size(axis)
    route = []
    for low in range(count):
        high = low | 1 << distance
        if high != low and high < count:
            route += [(low, high), (high, low)]
    return lax.ppermute(block, axis, route)


def fold_into(gathered):

    def add_rows(running, panel, offset):
        return jnp.dot(
            gathered, panel.reshape(panel.shape[0], -1), preferred_element_type=jnp.float32
        )

    return add_rows


def twiddle(my_index, level, row_count):
    span = 1 << level
    positions = my_index % span * row_count + jnp.arange(row_count, dtype=jnp.int32)
    angles = -TWO_PI / (2 * span * row_count) * positions.astype(jnp.float32)
    return (jnp.cos(angles)[:, None], jnp.sin(angles)[:, None])


def upper_flag(my_index, level):
    return my_index // (1 << level) % 2 == 1


def dft_tables(row_count):
    steps_idx = jnp.arange(row_count, dtype=jnp.int32)
    products = steps_idx[:, None] * steps_idx[None, :] % row_count
    angles = TWO_PI * products.astype(jnp.float32) / row_count
    return (jnp.cos(angles), jnp.sin(angles))


def forward_butterfly(signal):
    shard_count = lax.axis_size("seq")
    bit_count = shard_count.bit_length() - 1
    my_index = lax.axis_index("seq")
    row_count = signal.shape[0]
    top_level = bit_count - 1
    partner = swapped(signal, "seq", top_level)
    cos_t, sin_t = twiddle(my_index, top_level, row_count)
    upper_half = upper_flag(my_index, top_level)
    difference = partner - signal
    real_part = jnp.where(upper_half, difference * cos_t, signal + partner)
    imag_part = jnp.where(upper_half, difference * sin_t, jnp.zeros_like(signal))
    for level in range(top_level - 1, -1, -1):
        other_re, other_im = swapped((real_part, imag_part), "seq", level)
        cos_t, sin_t = twiddle(my_index, level, row_count)
        upper_half = upper_flag(my_index, level)
        diff_re = other_re - real_part
        diff_im = other_im - imag_part
        new_re = jnp.where(upper_half, diff_re * cos_t - diff_im * sin_t, real_part + other_re)
        new_im = jnp.where(upper_half, diff_re * sin_t + diff_im * cos_t, imag_part + other_im)
        real_part, imag_part = (new_re, new_im)
    cos_m, sin_m = dft_tables(row_count)
    matrix = jnp.concatenate(
        [jnp.concatenate([cos_m, sin_m], 1), jnp.concatenate([-sin_m, cos_m], 1)], 0
    )
    stacked = jnp.concatenate([real_part, imag_part], 0)
    spectrum = jnp.dot(matrix, stacked, precision=HIGHEST)
    return (spectrum[:row_count], spectrum[row_count:])


def spread_filter(filter_real, filter_imag):
    shard_count = lax.axis_size("seq")
    bit_count = shard_count.bit_length() - 1
    row_count, chan_width = filter_real.shape

    def reorder(table):
        split_bits = table.reshape((row_count // shard_count,) + (2,) * bit_count + (chan_width,))
        order = (0,) + tuple(range(bit_count, 0, -1)) + (bit_count + 1,)
        return jnp.transpose(split_bits, order).reshape(
            row_count // shard_count, shard_count, chan_width
        )

    got_re, got_im = (
        lax.all_to_all(reorder(filter_real), "seq", split_axis=1, concat_axis=0, tiled=True),
        lax.all_to_all(reorder(filter_imag), "seq", split_axis=1, concat_axis=0, tiled=True),
    )
    return (got_re.reshape(row_count, chan_width), got_im.reshape(row_count, chan_width))


def inverse_butterfly(spec_re, spec_im):
    shard_count = lax.axis_size("seq")
    bit_count = shard_count.bit_length() - 1
    my_index = lax.axis_index("seq")
    row_count = spec_re.shape[0]
    cos_m, sin_m = dft_tables(row_count)
    matrix = jnp.concatenate(
        [jnp.concatenate([cos_m, -sin_m], 1), jnp.concatenate([sin_m, cos_m], 1)], 0
    )
    stacked = jnp.dot(matrix, jnp.concatenate([spec_re, spec_im], 0), precision=HIGHEST) / row_count
    real_part = stacked[:row_count]
    imag_part = stacked[row_count:]
    for level in range(bit_count):
        other_re, other_im = swapped((real_part, imag_part), "seq", level)
        cos_t, sin_t = twiddle(my_index, level, row_count)
        upper_half = upper_flag(my_index, level)
        source_re = jnp.where(upper_half, real_part, other_re)
        source_im = jnp.where(upper_half, imag_part, other_im)
        base_re = jnp.where(upper_half, other_re, real_part)
        base_im = jnp.where(upper_half, other_im, imag_part)
        rotated_re = source_re * cos_t + source_im * sin_t
        rotated_im = source_im * cos_t - source_re * sin_t
        factor = jnp.where(upper_half, -0.5, 0.5)
        real_part = 0.5 * base_re + factor * rotated_re
        imag_part = 0.5 * base_im + factor * rotated_im
    return real_part


def shards(features, w_in, filter_real, filter_imag, skip_gain):
    gathered = lax.all_gather(features, "chan", axis=1, tiled=True)
    chan_width = w_in.shape[2]
    row_count = gathered.shape[0]
    add_rows = fold_into(gathered)
    zero_sum = jnp.zeros((row_count, 3 * chan_width), jnp.float32)
    projected = add_rows(zero_sum, lax.all_gather(w_in, "seq", axis=0, tiled=True), jnp.int32(0))
    input_gate = projected[:, :chan_width].astype(jnp.bfloat16)
    value_stream = projected[:, chan_width : 2 * chan_width].astype(jnp.bfloat16)
    output_gate = projected[:, 2 * chan_width :].astype(jnp.bfloat16)
    signal = input_gate.astype(jnp.float32) * value_stream.astype(jnp.float32)
    spec_re, spec_im = forward_butterfly(signal)
    resp_re, resp_im = spread_filter(filter_real, filter_imag)
    prod_re = resp_re * spec_re - resp_im * spec_im
    prod_im = resp_re * spec_im + resp_im * spec_re
    convolved = inverse_butterfly(prod_re, prod_im)
    result = output_gate.astype(jnp.float32) * (convolved + skip_gain[None, :] * signal)
    return result.astype(jnp.bfloat16)


def solution(mesh):
    placed = (
        P("seq", "chan"),
        P("seq", None, "chan"),
        P("seq", "chan"),
        P("seq", "chan"),
        P("chan"),
    )
    return jax.shard_map(
        shards, mesh=mesh, in_specs=placed, out_specs=P("seq", "chan"), check_vma=False
    )
```

profile of v0, /device:TPU:8, one launch (start us, length us, event | category | flops | bytes accessed | tf_op | source)
XLA Modules:
  0.0 783.1 jit_solution(4265865259562781646)
XLA Ops:
  8.0 326.5 %all-gather.5.cloned.1.call-done = bf16[4096,3,512]{2,0,1:T(8,128)(2,1)} async-done(((bf16[64,3,512]{2,0,1:T(8,128)(2,1)}), bf16[4096,3,512]{2,0,1:T(8,128)(2,1)}) %all-gather.5.cloned.1.call-update) | async-done | bytes 12582928 | tf_op jit(solution)/shard_map/all_gather | solution.py:133
  334.5 17.0 %copy.11 = bf16[4096,3,512]{0,2,1:T(8,128)(2,1)} copy(bf16[4096,3,512]{2,0,1:T(8,128)(2,1)} %all-gather.5.cloned.1.call-done) | data formatting | bytes 25165824 | tf_op jit(solution)/shard_map/all_gather | solution.py:133
  351.5 11.9 %all-gather.3.cloned.1.call-done = bf16[256,4096]{1,0:T(8,128)(2,1)} async-done(((bf16[256,1024]{1,0:T(8,128)(2,1)}), bf16[256,4096]{1,0:T(8,128)(2,1)}) %all-gather.3.cloned.1.call-update) | async-done | bytes 2097168 | tf_op jit(solution)/shard_map/all_gather | solution.py:128
  363.5 8.7 %convolution_convert_fusion = bf16[256,1536]{1,0:T(8,128)(2,1)S(1)} fusion(bf16[256,4096]{1,0:T(8,128)(2,1)} %all-gather.3.cloned.1.call-done, bf16[4096,1536]{0,1:T(8,128)(2,1)} %bitcast.17), kind=kOutput, calls=%fused_computation | convolution fusion | flops 3221618688 | bytes 15466496 | tf_op jit(solution)/shard_map/dot_general | solution.py:25
  372.2 1.5 collective-permute-start
  373.8 12.6 %collective-permute-done = f32[256,512]{1,0:T(8,128)S(1)} collective-permute-done((f32[256,512]{1,0:T(8,128)S(1)}, f32[256,512]{1,0:T(8,128)S(1)}, u32[]{:S(2)}, u32[]{:S(2)}) %collective-permute-start) | collective-permute-done | bytes 524320 | tf_op jit(solution)/shard_map/ppermute | solution.py:19
  386.5 5.8 collective-permute-start.1
  392.6 18.5 %collective-permute-done.1 = f32[256,512]{1,0:T(8,128)S(1)} collective-permute-done((f32[256,512]{1,0:T(8,128)S(1)}, f32[256,512]{1,0:T(8,128)S(1)}, u32[]{:S(2)}, u32[]{:S(2)}) %collective-permute-start.1) | collective-permute-done | bytes 524320 | tf_op jit(solution)/shard_map/ppermute | solution.py:19
  411.1 25.9 %collective-permute-done.2 = f32[256,512]{1,0:T(8,128)S(1)} collective-permute-done((f32[256,512]{1,0:T(8,128)S(1)}, f32[256,512]{1,0:T(8,128)S(1)}, u32[]{:S(2)}, u32[]{:S(2)}) %collective-permute-start.2) | collective-permute-done | bytes 524320 | tf_op jit(solution)/shard_map/ppermute | solution.py:19
  437.1 0.8 copy-done.3
  437.9 1.3 add_select_fusion.9
  439.2 3.2 collective-permute-start.3
  442.5 34.0 %collective-permute-done.3 = f32[256,512]{1,0:T(8,128)S(1)} collective-permute-done((f32[256,512]{1,0:T(8,128)S(1)}, f32[256,512]{1,0:T(8,128)S(1)}, u32[]{:S(2)}, u32[]{:S(2)}) %collective-permute-start.3) | collective-permute-done | bytes 524320 | tf_op jit(solution)/shard_map/ppermute | solution.py:19
  476.5 11.2 %collective-permute-done.4 = f32[256,512]{1,0:T(8,128)S(1)} collective-permute-done((f32[256,512]{1,0:T(8,128)S(1)}, f32[256,512]{1,0:T(8,128)S(1)}, u32[]{:S(2)}, u32[]{:S(2)}) %collective-permute-start.4) | collective-permute-done | bytes 524320 | tf_op jit(solution)/shard_map/ppermute | solution.py:19
  487.6 0.8 copy-done.4
  488.4 1.3 add_select_fusion.7
  489.8 2.0 collective-permute-start.6
  491.9 1.3 reshape.84
  493.2 1.2 copy.12
  494.4 8.3 %all-to-all-start = ((f32[4,64,512]{2,0,1:T(4,128)}), f32[4,64,512]{2,0,1:T(4,128)S(1)}, u32[]{:S(2)}, u32[]{:S(2)}) async-start(f32[4,64,512]{2,0,1:T(4,128)} %bitcast.2), calls=%async_computation | async-start | bytes 1048576 | tf_op jit(solution)/shard_map/all_to_all | solution.py:93
  502.8 3.2 collective-permute-done.5
  505.9 13.4 %collective-permute-done.6 = f32[256,512]{1,0:T(8,128)S(1)} collective-permute-done((f32[256,512]{1,0:T(8,128)S(1)}, f32[256,512]{1,0:T(8,128)S(1)}, u32[]{:S(2)}, u32[]{:S(2)}) %collective-permute-start.6) | collective-permute-done | bytes 524320 | tf_op jit(solution)/shard_map/ppermute | solution.py:19
  520.1 1.5 add_select_fusion.5
  521.6 3.2 collective-permute-start.7
  525.2 1.3 reshape.87
  526.6 1.1 copy.13
  527.7 3.0 all-to-all-done
  530.7 6.3 all-to-all-start.1
  537.1 2.1 collective-permute-done.7
  539.2 14.6 %collective-permute-done.8 = f32[256,512]{1,0:T(8,128)} collective-permute-done((f32[256,512]{1,0:T(8,128)S(1)}, f32[256,512]{1,0:T(8,128)}, u32[]{:S(2)}, u32[]{:S(2)}) %collective-permute-start.8) | collective-permute-done | bytes 524320 | tf_op jit(solution)/shard_map/ppermute | solution.py:19
  553.8 2.3 add_select_fusion.3
  556.6 1.6 collective-permute-start.9
  558.2 1.7 fusion.23
  559.8 1.8 fusion.21
  562.0 9.2 %collective-permute-done.10 = f32[256,512]{1,0:T(8,128)S(1)} collective-permute-done((f32[256,512]{1,0:T(8,128)}, f32[256,512]{1,0:T(8,128)S(1)}, u32[]{:S(2)}, u32[]{:S(2)}) %collective-permute-start.10) | collective-permute-done | bytes 524320 | tf_op jit(solution)/shard_map/ppermute | solution.py:19
  571.2 7.3 collective-permute-done.9
  578.4 1.5 add_select_fusion.1
  579.9 3.0 fusion.3
  583.2 3.0 convolution_multiply_fusion
  587.0 1.5 collective-permute-start.12
  588.4 12.8 %collective-permute-done.11 = f32[256,512]{1,0:T(8,128)S(1)} collective-permute-done((f32[256,512]{1,0:T(8,128)S(1)}, f32[256,512]{1,0:T(8,128)S(1)}, u32[]{:S(2)}, u32[]{:S(2)}) %collective-permute-start.11) | collective-permute-done | bytes 524320 | tf_op jit(solution)/shard_map/ppermute | solution.py:19
  601.3 6.4 collective-permute-done.12
  607.6 1.4 multiply_add_fusion.9
  609.0 3.9 collective-permute-start.13
  613.3 12.5 %collective-permute-done.13 = f32[256,512]{1,0:T(8,128)S(1)} collective-permute-done((f32[256,512]{1,0:T(8,128)S(1)}, f32[256,512]{1,0:T(8,128)S(1)}, u32[]{:S(2)}, u32[]{:S(2)}) %collective-permute-start.13) | collective-permute-done | bytes 524320 | tf_op jit(solution)/shard_map/ppermute | solution.py:19
  625.8 7.2 collective-permute-done.14
  633.0 1.4 multiply_add_fusion.7
  634.3 0.9 collective-permute-start.15
  635.2 1.2 collective-permute-start.16
  636.5 12.8 %collective-permute-done.15 = f32[256,512]{1,0:T(8,128)S(1)} collective-permute-done((f32[256,512]{1,0:T(8,128)S(1)}, f32[256,512]{1,0:T(8,128)S(1)}, u32[]{:S(2)}, u32[]{:S(2)}) %collective-permute-start.15) | collective-permute-done | bytes 524320 | tf_op jit(solution)/shard_map/ppermute | solution.py:19
  649.3 6.3 collective-permute-done.16
  655.6 1.4 multiply_add_fusion.5
  657.0 2.9 collective-permute-start.18
  659.9 30.0 %collective-permute-done.17 = f32[256,512]{1,0:T(8,128)S(1)} collective-permute-done((f32[256,512]{1,0:T(8,128)S(1)}, f32[256,512]{1,0:T(8,128)S(1)}, u32[]{:S(2)}, u32[]{:S(2)}) %collective-permute-start.17) | collective-permute-done | bytes 524320 | tf_op jit(solution)/shard_map/ppermute | solution.py:19
  690.0 10.7 %collective-permute-done.18 = f32[256,512]{1,0:T(8,128)} collective-permute-done((f32[256,512]{1,0:T(8,128)S(1)}, f32[256,512]{1,0:T(8,128)}, u32[]{:S(2)}, u32[]{:S(2)}) %collective-permute-start.18) | collective-permute-done | bytes 524320 | tf_op jit(solution)/shard_map/ppermute | solution.py:19
  700.7 1.4 multiply_add_fusion.3
  702.2 5.9 collective-permute-start.20
  708.1 32.6 %collective-permute-done.19 = f32[256,512]{1,0:T(8,128)S(1)} collective-permute-done((f32[256,512]{1,0:T(8,128)S(1)}, f32[256,512]{1,0:T(8,128)S(1)}, u32[]{:S(2)}, u32[]{:S(2)}) %collective-permute-start.19) | collective-permute-done | bytes 524320 | tf_op jit(solution)/shard_map/ppermute | solution.py:19
  740.6 9.7 %collective-permute-done.20 = f32[256,512]{1,0:T(8,128)} collective-permute-done((f32[256,512]{1,0:T(8,128)S(1)}, f32[256,512]{1,0:T(8,128)}, u32[]{:S(2)}, u32[]{:S(2)}) %collective-permute-start.20) | collective-permute-done | bytes 524320 | tf_op jit(solution)/shard_map/ppermute | solution.py:19
  750.4 1.4 multiply_add_fusion.1
  751.8 2.0 collective-permute-start.22
  753.9 12.8 %collective-permute-done.21 = f32[256,512]{1,0:T(8,128)S(1)} collective-permute-done((f32[256,512]{1,0:T(8,128)S(1)}, f32[256,512]{1,0:T(8,128)S(1)}, u32[]{:S(2)}, u32[]{:S(2)}) %collective-permute-start.21) | collective-permute-done | bytes 524320 | tf_op jit(solution)/shard_map/ppermute | solution.py:19
  766.7 8.5 %collective-permute-done.22 = f32[256,512]{1,0:T(8,128)S(1)} collective-permute-done((f32[256,512]{1,0:T(8,128)S(1)}, f32[256,512]{1,0:T(8,128)S(1)}, u32[]{:S(2)}, u32[]{:S(2)}) %collective-permute-start.22) | collective-permute-done | bytes 524320 | tf_op jit(solution)/shard_map/ppermute | solution.py:19
  775.2 1.0 multiply_convert_fusion
  (37 shorter events, 5.9 us)
Async XLA Ops:
  6.5 328.0 %all-gather.5.cloned.1.call-start = ((), (), s32[]{:S(2)}) async-start(), calls=%async_computation.3 | async-start | bytes 12779520 | tf_op jit(solution)/shard_map/all_gather | solution.py:133
  7.3 356.2 %all-gather.3.cloned.1.call-start = ((), (), s32[]{:S(2)}) async-start(), calls=%async_computation.2 | async-start | bytes 2621440 | tf_op jit(solution)/shard_map/all_gather | solution.py:128
  372.2 14.2 %collective-permute-start = (f32[256,512]{1,0:T(8,128)S(1)}, f32[256,512]{1,0:T(8,128)S(1)}, u32[]{:S(2)}, u32[]{:S(2)}) collective-permute-start(f32[256,512]{1,0:T(8,128)S(1)} %convert_multiply_fusion), channel_id=1, source_target_pairs={{0,128},{128,0},{4,132},{132,4},{8,136},{136,8},{12,140},{140,12},... | collective-permute-start | bytes 1572872 | tf_op jit(solution)/shard_map/ppermute | solution.py:19
  386.5 24.6 %collective-permute-start.1 = (f32[256,512]{1,0:T(8,128)S(1)}, f32[256,512]{1,0:T(8,128)S(1)}, u32[]{:S(2)}, u32[]{:S(2)}) collective-permute-start(f32[256,512]{1,0:T(8,128)S(1)} %get-tuple-element.27), channel_id=1, source_target_pairs={{0,64},{64,0},{4,68},{68,4},{8,72},{72,8},{12,76},{76,12},{16,80},... | collective-permute-start | bytes 1572872 | tf_op jit(solution)/shard_map/ppermute | solution.py:19
  392.4 44.7 %collective-permute-start.2 = (f32[256,512]{1,0:T(8,128)S(1)}, f32[256,512]{1,0:T(8,128)S(1)}, u32[]{:S(2)}, u32[]{:S(2)}) collective-permute-start(f32[256,512]{1,0:T(8,128)S(1)} %get-tuple-element.28), channel_id=1, source_target_pairs={{0,64},{64,0},{4,68},{68,4},{8,72},{72,8},{12,76},{76,12},{16,80},... | collective-permute-start | bytes 1572872 | tf_op jit(solution)/shard_map/ppermute | solution.py:19
  437.1 0.8 copy-start.3
  439.2 37.3 %collective-permute-start.3 = (f32[256,512]{1,0:T(8,128)S(1)}, f32[256,512]{1,0:T(8,128)S(1)}, u32[]{:S(2)}, u32[]{:S(2)}) collective-permute-start(f32[256,512]{1,0:T(8,128)S(1)} %get-tuple-element.23), channel_id=1, source_target_pairs={{0,32},{32,0},{4,36},{36,4},{8,40},{40,8},{12,44},{44,12},{16,48},... | collective-permute-start | bytes 1572872 | tf_op jit(solution)/shard_map/ppermute | solution.py:19
  442.3 45.3 %collective-permute-start.4 = (f32[256,512]{1,0:T(8,128)S(1)}, f32[256,512]{1,0:T(8,128)S(1)}, u32[]{:S(2)}, u32[]{:S(2)}) collective-permute-start(f32[256,512]{1,0:T(8,128)S(1)} %get-tuple-element.24), channel_id=1, source_target_pairs={{0,32},{32,0},{4,36},{36,4},{8,40},{40,8},{12,44},{44,12},{16,48},... | collective-permute-start | bytes 1572872 | tf_op jit(solution)/shard_map/ppermute | solution.py:19
  487.6 0.8 copy-start.4
  489.7 16.2 %collective-permute-start.5 = (f32[256,512]{1,0:T(8,128)S(1)}, f32[256,512]{1,0:T(8,128)S(1)}, u32[]{:S(2)}, u32[]{:S(2)}) collective-permute-start(f32[256,512]{1,0:T(8,128)S(1)} %get-tuple-element.21), channel_id=1, source_target_pairs={{0,16},{16,0},{4,20},{20,4},{8,24},{24,8},{12,28},{28,12},{32,48},... | collective-permute-start | bytes 1572872 | tf_op jit(solution)/shard_map/ppermute | solution.py:19
  489.8 29.5 %collective-permute-start.6 = (f32[256,512]{1,0:T(8,128)S(1)}, f32[256,512]{1,0:T(8,128)S(1)}, u32[]{:S(2)}, u32[]{:S(2)}) collective-permute-start(f32[256,512]{1,0:T(8,128)S(1)} %get-tuple-element.22), channel_id=1, source_target_pairs={{0,16},{16,0},{4,20},{20,4},{8,24},{24,8},{12,28},{28,12},{32,48},... | collective-permute-start | bytes 1572872 | tf_op jit(solution)/shard_map/ppermute | solution.py:19
  494.4 36.4 %all-to-all-start = ((f32[4,64,512]{2,0,1:T(4,128)}), f32[4,64,512]{2,0,1:T(4,128)S(1)}, u32[]{:S(2)}, u32[]{:S(2)}) async-start(f32[4,64,512]{2,0,1:T(4,128)} %bitcast.2), calls=%async_computation | async-start | bytes 1048576 | tf_op jit(solution)/shard_map/all_to_all | solution.py:93
  505.9 13.4 %copy-start.1 = (f32[256,512]{1,0:T(8,128)}, f32[256,512]{1,0:T(8,128)S(1)}, u32[]{:S(2)}) copy-start(f32[256,512]{1,0:T(8,128)S(1)} %collective-permute-done.5) | copy-start | bytes 1572868
  519.3 0.8 copy-start.2
  521.6 17.6 %collective-permute-start.7 = (f32[256,512]{1,0:T(8,128)S(1)}, f32[256,512]{1,0:T(8,128)S(1)}, u32[]{:S(2)}, u32[]{:S(2)}) collective-permute-start(f32[256,512]{1,0:T(8,128)S(1)} %get-tuple-element.19), channel_id=1, source_target_pairs={{0,8},{8,0},{4,12},{12,4},{16,24},{24,16},{20,28},{28,20},{32,40},... | collective-permute-start | bytes 1572872 | tf_op jit(solution)/shard_map/ppermute | solution.py:19
  524.8 29.0 %collective-permute-start.8 = (f32[256,512]{1,0:T(8,128)S(1)}, f32[256,512]{1,0:T(8,128)}, u32[]{:S(2)}, u32[]{:S(2)}) collective-permute-start(f32[256,512]{1,0:T(8,128)S(1)} %get-tuple-element.20), channel_id=1, source_target_pairs={{0,8},{8,0},{4,12},{12,4},{16,24},{24,16},{20,28},{28,20},{32,40},... | collective-permute-start | bytes 1572872 | tf_op jit(solution)/shard_map/ppermute | solution.py:19
  530.7 31.1 %all-to-all-start.1 = ((f32[4,64,512]{2,0,1:T(4,128)}), f32[4,64,512]{2,0,1:T(4,128)S(1)}, u32[]{:S(2)}, u32[]{:S(2)}) async-start(f32[4,64,512]{2,0,1:T(4,128)} %bitcast.6), calls=%async_computation.1 | async-start | bytes 1048576 | tf_op jit(solution)/shard_map/all_to_all | solution.py:94
  539.2 14.6 %copy-start = (f32[256,512]{1,0:T(8,128)}, f32[256,512]{1,0:T(8,128)S(1)}, u32[]{:S(2)}) copy-start(f32[256,512]{1,0:T(8,128)S(1)} %collective-permute-done.7) | copy-start | bytes 1572868
  556.1 15.1 %collective-permute-start.10 = (f32[256,512]{1,0:T(8,128)}, f32[256,512]{1,0:T(8,128)S(1)}, u32[]{:S(2)}, u32[]{:S(2)}) collective-permute-start(f32[256,512]{1,0:T(8,128)} %get-tuple-element.18), channel_id=1, source_target_pairs={{0,4},{4,0},{8,12},{12,8},{16,20},{20,16},{24,28},{28,24},{32,36},... | collective-permute-start | bytes 1572872 | tf_op jit(solution)/shard_map/ppermute | solution.py:19
  556.6 21.9 %collective-permute-start.9 = (f32[256,512]{1,0:T(8,128)S(1)}, f32[256,512]{1,0:T(8,128)}, u32[]{:S(2)}, u32[]{:S(2)}) collective-permute-start(f32[256,512]{1,0:T(8,128)S(1)} %get-tuple-element.17), channel_id=1, source_target_pairs={{0,4},{4,0},{8,12},{12,8},{16,20},{20,16},{24,28},{28,24},{32,36},... | collective-permute-start | bytes 1572872 | tf_op jit(solution)/shard_map/ppermute | solution.py:19
  583.0 192.3 %copy-start.5 = (f32[512]{0:T(512)S(1)}, f32[512]{0:T(512)}, u32[]{:S(2)}) copy-start(f32[512]{0:T(512)} %param.9) | copy-start | bytes 6148
  586.3 14.9 %collective-permute-start.11 = (f32[256,512]{1,0:T(8,128)S(1)}, f32[256,512]{1,0:T(8,128)S(1)}, u32[]{:S(2)}, u32[]{:S(2)}) collective-permute-start(f32[256,512]{1,0:T(8,128)S(1)} %get-tuple-element.29), channel_id=1, source_target_pairs={{0,4},{4,0},{8,12},{12,8},{16,20},{20,16},{24,28},{28,24},{32,36},... | collective-permute-start | bytes 1572872 | tf_op jit(solution)/shard_map/ppermute | solution.py:19
  587.0 20.7 %collective-permute-start.12 = (f32[256,512]{1,0:T(8,128)S(1)}, f32[256,512]{1,0:T(8,128)}, u32[]{:S(2)}, u32[]{:S(2)}) collective-permute-start(f32[256,512]{1,0:T(8,128)S(1)} %get-tuple-element.30), channel_id=1, source_target_pairs={{0,4},{4,0},{8,12},{12,8},{16,20},{20,16},{24,28},{28,24},{32,36},... | collective-permute-start | bytes 1572872 | tf_op jit(solution)/shard_map/ppermute | solution.py:19
  609.0 16.8 %collective-permute-start.13 = (f32[256,512]{1,0:T(8,128)S(1)}, f32[256,512]{1,0:T(8,128)S(1)}, u32[]{:S(2)}, u32[]{:S(2)}) collective-permute-start(f32[256,512]{1,0:T(8,128)S(1)} %get-tuple-element.13), channel_id=1, source_target_pairs={{0,8},{8,0},{4,12},{12,4},{16,24},{24,16},{20,28},{28,20},{32,40},... | collective-permute-start | bytes 1572872 | tf_op jit(solution)/shard_map/ppermute | solution.py:19
  612.9 20.0 %collective-permute-start.14 = (f32[256,512]{1,0:T(8,128)S(1)}, f32[256,512]{1,0:T(8,128)}, u32[]{:S(2)}, u32[]{:S(2)}) collective-permute-start(f32[256,512]{1,0:T(8,128)S(1)} %get-tuple-element.14), channel_id=1, source_target_pairs={{0,8},{8,0},{4,12},{12,4},{16,24},{24,16},{20,28},{28,20},{32,40},... | collective-permute-start | bytes 1572872 | tf_op jit(solution)/shard_map/ppermute | solution.py:19
  634.3 14.9 %collective-permute-start.15 = (f32[256,512]{1,0:T(8,128)S(1)}, f32[256,512]{1,0:T(8,128)S(1)}, u32[]{:S(2)}, u32[]{:S(2)}) collective-permute-start(f32[256,512]{1,0:T(8,128)S(1)} %get-tuple-element.11), channel_id=1, source_target_pairs={{0,16},{16,0},{4,20},{20,4},{8,24},{24,8},{12,28},{28,12},{32,48},... | collective-permute-start | bytes 1572872 | tf_op jit(solution)/shard_map/ppermute | solution.py:19
  635.2 20.4 %collective-permute-start.16 = (f32[256,512]{1,0:T(8,128)S(1)}, f32[256,512]{1,0:T(8,128)}, u32[]{:S(2)}, u32[]{:S(2)}) collective-permute-start(f32[256,512]{1,0:T(8,128)S(1)} %get-tuple-element.12), channel_id=1, source_target_pairs={{0,16},{16,0},{4,20},{20,4},{8,24},{24,8},{12,28},{28,12},{32,48},... | collective-permute-start | bytes 1572872 | tf_op jit(solution)/shard_map/ppermute | solution.py:19
  656.9 33.0 %collective-permute-start.17 = (f32[256,512]{1,0:T(8,128)S(1)}, f32[256,512]{1,0:T(8,128)S(1)}, u32[]{:S(2)}, u32[]{:S(2)}) collective-permute-start(f32[256,512]{1,0:T(8,128)S(1)} %get-tuple-element.9), channel_id=1, source_target_pairs={{0,32},{32,0},{4,36},{36,4},{8,40},{40,8},{12,44},{44,12},{16,48},... | collective-permute-start | bytes 1572872 | tf_op jit(solution)/shard_map/ppermute | solution.py:19
  657.0 43.7 %collective-permute-start.18 = (f32[256,512]{1,0:T(8,128)S(1)}, f32[256,512]{1,0:T(8,128)}, u32[]{:S(2)}, u32[]{:S(2)}) collective-permute-start(f32[256,512]{1,0:T(8,128)S(1)} %get-tuple-element.10), channel_id=1, source_target_pairs={{0,32},{32,0},{4,36},{36,4},{8,40},{40,8},{12,44},{44,12},{16,48},... | collective-permute-start | bytes 1572872 | tf_op jit(solution)/shard_map/ppermute | solution.py:19
  702.1 38.6 %collective-permute-start.19 = (f32[256,512]{1,0:T(8,128)S(1)}, f32[256,512]{1,0:T(8,128)S(1)}, u32[]{:S(2)}, u32[]{:S(2)}) collective-permute-start(f32[256,512]{1,0:T(8,128)S(1)} %get-tuple-element.7), channel_id=1, source_target_pairs={{0,64},{64,0},{4,68},{68,4},{8,72},{72,8},{12,76},{76,12},{16,80},... | collective-permute-start | bytes 1572872 | tf_op jit(solution)/shard_map/ppermute | solution.py:19
  702.2 48.2 %collective-permute-start.20 = (f32[256,512]{1,0:T(8,128)S(1)}, f32[256,512]{1,0:T(8,128)}, u32[]{:S(2)}, u32[]{:S(2)}) collective-permute-start(f32[256,512]{1,0:T(8,128)S(1)} %get-tuple-element.8), channel_id=1, source_target_pairs={{0,64},{64,0},{4,68},{68,4},{8,72},{72,8},{12,76},{76,12},{16,80},... | collective-permute-start | bytes 1572872 | tf_op jit(solution)/shard_map/ppermute | solution.py:19
  751.7 14.9 %collective-permute-start.21 = (f32[256,512]{1,0:T(8,128)S(1)}, f32[256,512]{1,0:T(8,128)S(1)}, u32[]{:S(2)}, u32[]{:S(2)}) collective-permute-start(f32[256,512]{1,0:T(8,128)S(1)} %get-tuple-element.5), channel_id=1, source_target_pairs={{0,128},{128,0},{4,132},{132,4},{8,136},{136,8},{12,140},{140,12},... | collective-permute-start | bytes 1572872 | tf_op jit(solution)/shard_map/ppermute | solution.py:19
  751.8 23.4 %collective-permute-start.22 = (f32[256,512]{1,0:T(8,128)S(1)}, f32[256,512]{1,0:T(8,128)S(1)}, u32[]{:S(2)}, u32[]{:S(2)}) collective-permute-start(f32[256,512]{1,0:T(8,128)S(1)} %get-tuple-element.6), channel_id=1, source_target_pairs={{0,128},{128,0},{4,132},{132,4},{8,136},{136,8},{12,140},{140,12},... | collective-permute-start | bytes 1572872 | tf_op jit(solution)/shard_map/ppermute | solution.py:19
Sparse Core Ops, SparseCore 0:
  9.1 325.3 all-gather.4
  336.3 27.0 all-gather.2
where the time goes:
time: 795 us; the launch traced here: 783 us
  waiting for transfers between devices  657 us (83%)
  starting transfers between devices  52.8 us (7%)
  local copies, waits for them, and re-layouts  24.8 us (3%)
  other arithmetic  19.8 us (2%)
  matrix products  14.7 us (2%)
  between operations  13.7 us (2%)
    all_gather x1, waiting for transfers between devices, shards(): lax.all_gather(w_in, 'seq', axis=0, tiled=True)  327 us
    ppermute x23, waiting for transfers between devices, swapped(): return lax.ppermute(block, axis, route)  314 us
    ppermute x23, starting transfers between devices, swapped(): return lax.ppermute(block, axis, route)  38.2 us
    all_gather x1, local copies, waits for them, and re-layouts, shards(): lax.all_gather(w_in, 'seq', axis=0, tiled=True)  17 us
  transfers between devices with their start and end apart: 27, of which 26 were waited for; matrix products, arithmetic and copies ran while one was open for 4% of the time, Pallas kernels for 0%

commit v1 on v0

v1 whole, which is shorter than its diff:
```python
import functools

import jax
import jax.numpy as jnp
import numpy as np
from jax import lax
from jax.experimental import pallas as pl
from jax.experimental.pallas import tpu as pltpu
from jax.sharding import Mesh
from jax.sharding import PartitionSpec as P

MESH = pl.DeviceIdType.MESH
F32 = jnp.float32
BF16 = jnp.bfloat16

YL, NZ, NX, YH, NC = 2, 8, 4, 2, 2
NS = YL * NZ * NX
Q = YL * NZ
ROWS = 256
HALF = ROWS // 2
DBLK = 1024
LANES = 128
CB = 8
N1 = 128
WROWS = 64 * NX
COLS = 3 * LANES


def split16(table):
    high = table.astype(BF16)
    return high, (table - high.astype(F32)).astype(BF16)


def tables():
    index = np.arange(N1)
    angle = 2.0 * np.pi * ((index[:, None] * index[None, :]) % N1) / N1
    cos, sin = np.cos(angle), np.sin(angle)
    twist = 2.0 * np.pi * (index[:, None] * index[None, :]) / (N1 * N1)

    def pair(table):
        high = table.astype(np.float32).astype(jnp.bfloat16)
        low = (table - high.astype(np.float64)).astype(np.float32).astype(jnp.bfloat16)
        return high, low

    first = pair(np.concatenate([cos, -sin], 0))
    first = np.concatenate(first, 1)
    forward = np.concatenate(pair(np.block([[cos, sin], [-sin, cos]])), 0)
    back = np.concatenate(pair(np.block([[cos, -sin], [sin, cos]])), 0)
    last = np.concatenate(pair(np.concatenate([cos, -sin], 1) / (N1 * N1)), 0)
    return (
        first,
        forward,
        back,
        last,
        np.cos(twist).astype(np.float32),
        np.sin(twist).astype(np.float32),
    )


def dot(a, b):
    return jnp.dot(a, b, preferred_element_type=F32)


def dot_nt(a, b):
    return lax.dot_general(a, b, (((1,), (1,)), ((), ())), preferred_element_type=F32)


def three_pass(product, stacked, value):
    m = stacked.shape[0] // 2
    high, low = split16(value)
    both = product(stacked, high)
    return both[:m] + both[m:] + product(stacked[:m], low)


def kernel(
    feat_ref,
    w_ref,
    fre_ref,
    fim_ref,
    skip_ref,
    first_ref,
    forward_ref,
    back_ref,
    last_ref,
    tc_ref,
    ts_ref,
    out_ref,
    feat,
    wbuf,
    hmsg,
    hbuf,
    sigmsg,
    xs,
    gmsg,
    gbuf,
    ybf,
    ybuf,
    xf,
    yf,
    hre,
    him,
    f_send,
    f_recv,
    w_send,
    ws_recv,
    w_recv,
    g_send,
    g_recv,
    bulk_send,
    bulk_recv,
    local_sem,
):
    yl = lax.axis_index("y_lo")
    z = lax.axis_index("z")
    x = lax.axis_index("x")
    yh = lax.axis_index("y_hi")
    core = lax.axis_index("core")
    q = yl * NZ + z
    me_s = q * NX + x
    me_m = x * Q + q

    def wrap(value, count):
        return lax.rem(value + count, count)

    def at_x(step):
        return {"x": wrap(x + step, NX)}

    def at_z(step):
        return {"z": wrap(z + step, NZ)}

    over_yl, over_yh, over_core = {"y_lo": 1 - yl}, {"y_hi": 1 - yh}, {"core": 1 - core}

    def peer(step):
        m = lax.rem(me_m + step, NS)
        px, pq = m // Q, lax.rem(m, Q)
        return m, pq * NX + px, {"x": px, "y_lo": pq // NZ, "z": lax.rem(pq, NZ)}

    barrier = pltpu.get_barrier_semaphore()

    def greet(step, carry):
        _, _, where = peer(step)
        pl.semaphore_signal(barrier, inc=1, device_id=where, device_id_type=MESH)
        return carry

    lax.fori_loop(1, NS, greet, 0)
    pl.semaphore_signal(barrier, inc=1, device_id=over_yh, device_id_type=MESH)
    pl.semaphore_signal(barrier, inc=1, device_id=over_core, device_id_type=MESH)
    pl.semaphore_wait(barrier, NS + 1)

    started = []

    def w_block(dz, dyl):
        return wbuf.at[(yl if dyl == 0 else 1 - yl) * NZ + wrap(z + dz, NZ)]

    def w_go(src, dst, recv_sem, where):
        index = len([1 for kind, _ in started if kind == "w"])
        copy = pltpu.make_async_remote_copy(
            src_ref=src,
            dst_ref=dst,
            send_sem=w_send.at[index],
            recv_sem=recv_sem,
            device_id=where,
            device_id_type=MESH,
        )
        copy.start()
        started.append(("w", copy))

    def w_await(dst, recv_sem):
        pltpu.make_async_remote_copy(
            src_ref=dst,
            dst_ref=dst,
            send_sem=w_send.at[0],
            recv_sem=recv_sem,
            device_id=over_core,
            device_id_type=MESH,
        ).wait_recv()

    def w_slot(dx):
        return wbuf.at[q, pl.ds(pl.multiple_of(wrap(x + dx, NX) * 64, 64), 64)]

    own_w = pltpu.make_async_copy(w_ref.at[x], w_slot(0), local_sem.at[0])
    own_w.start()
    for step in (1, 3, 2):
        w_go(w_ref.at[wrap(x + step, NX)], w_slot(0), ws_recv.at[3 - step], at_x(step))

    def f_block(dx, dyh, dc, h):
        column = (yh if dyh == 0 else 1 - yh) * NC + (core if dc == 0 else 1 - core)
        return feat.at[wrap(x + dx, NX), column, pl.ds(h * HALF, HALF)]

    def f_sem(dx, dyh, dc, h):
        return f_recv.at[((dx % NX * 2 + dyh) * 2 + dc) * 2 + h]

    def f_go(src, block, here, where):
        dx, dyh, dc, h = here
        index = len([1 for kind, _ in started if kind == "f"])
        copy = pltpu.make_async_remote_copy(
            src_ref=src,
            dst_ref=block,
            send_sem=f_send.at[index],
            recv_sem=f_sem(dx, dyh, dc, h),
            device_id=where,
            device_id_type=MESH,
        )
        copy.start()
        started.append(("f", copy))

    def f_await(dx, dyh, dc, h):
        block = f_block(dx, dyh, dc, h)
        pltpu.make_async_remote_copy(
            src_ref=block,
            dst_ref=block,
            send_sem=f_send.at[0],
            recv_sem=f_sem(dx, dyh, dc, h),
            device_id=over_core,
            device_id_type=MESH,
        ).wait_recv()

    for h in range(2):
        src = feat_ref.at[pl.ds(h * HALF, HALF)]
        block = f_block(0, 0, 0, h)
        f_go(src, block, (3, 0, 0, h), at_x(1))
        f_go(src, block, (1, 0, 0, h), at_x(-1))
        f_go(src, block, (0, 1, 0, h), over_yh)
        f_go(src, block, (0, 0, 1, h), over_core)
    own_f = pltpu.make_async_copy(feat_ref, feat.at[x, yh * NC + core], local_sem.at[1])
    own_f.start()

    def forward_f(dx, dyh, h):
        f_await(dx, dyh, 0, h)
        block = f_block(dx, dyh, 0, h)
        if dx == 0:
            f_go(block, block, (3, dyh, 0, h), at_x(1))
            f_go(block, block, (1, dyh, 0, h), at_x(-1))
        if dx == 3 and h == 0:
            f_go(block, block, (2, dyh, 0, h), at_x(1))
        if dx == 1 and h == 1:
            f_go(block, block, (2, dyh, 0, h), at_x(-1))
        f_go(block, block, (dx, dyh, 1, h), over_core)

    def w_sem(dz, dyl):
        return w_recv.at[dz % NZ * 2 + dyl]

    def forward_w(dz, dyl):
        block = w_block(dz, dyl)
        if (dz, dyl) == (0, 0):
            own_w.wait()
            for step in range(3):
                w_await(w_slot(1 + step), ws_recv.at[step])
            w_go(block, block, w_sem(0, 1), over_yl)
        else:
            w_await(block, w_sem(dz, dyl))
        if -3 < dz <= 0 or (dz == -3 and dyl == 0):
            w_go(block, block, w_sem(dz - 1, dyl), at_z(1))
        if 0 <= dz < 3 or (dz == 3 and dyl == 1):
            w_go(block, block, w_sem(dz + 1, dyl), at_z(-1))

    def filter_rows(part, ref, chunk):
        lanes = pl.ds(pl.multiple_of(chunk * LANES, LANES), LANES)
        block = ref[:, lanes]
        if part == 0:
            block = block + skip_ref[:, lanes]
        turned = block.T
        parts = [turned[:, i * N1 : (i + 1) * N1].reshape(Q, 1, CB, N1) for i in range(2)]
        stacked = jnp.concatenate(parts, 1).reshape(Q, 2 * CB, N1)
        hmsg[pl.ds(chunk * Q, Q), part] = stacked.astype(BF16)

    def filter_chunk(chunk, carry):
        filter_rows(0, fre_ref, chunk)
        filter_rows(1, fim_ref, chunk)
        return carry

    forward_w(0, 0)
    lax.fori_loop(0, NX, filter_chunk, 0)
    forward_w(0, 1)
    own_rows = pl.ds(pl.multiple_of(me_s * 2 * CB, 2 * CB), 2 * CB)

    def h_copy(m, where):
        return pltpu.make_async_remote_copy(
            src_ref=hmsg.at[m],
            dst_ref=hbuf.at[:, own_rows],
            send_sem=bulk_send.at[0],
            recv_sem=bulk_recv.at[0],
            device_id=where,
            device_id_type=MESH,
        )

    def send_h(step, carry):
        m, _, where = peer(step)
        h_copy(m, where).start()
        return carry

    lax.fori_loop(1, NS, send_h, 0)
    own_h = pltpu.make_async_copy(hmsg.at[me_m], hbuf.at[:, own_rows], local_sem.at[2])
    own_h.start()

    for dx in (3, 1):
        forward_f(dx, 0, 0)
    for dz in (-1, 1):
        forward_w(dz, 0)
    for dx in (3, 1):
        forward_f(dx, 0, 1)
    for dz in (-1, 1):
        forward_w(dz, 1)
    forward_f(0, 1, 0)
    for dyl in (0, 1):
        for dz in (-2, 2):
            forward_w(dz, dyl)
    forward_f(0, 1, 1)
    for h in (0, 1):
        for dx in (3, 1):
            forward_f(dx, 1, h)
    for dyl in (0, 1):
        for dz in (-3, 3):
            forward_w(dz, dyl)
    for dyh in (0, 1):
        for h in (0, 1):
            forward_f(2, dyh, h)
    w_await(w_block(-4, 0), w_sem(-4, 0))
    w_await(w_block(4, 1), w_sem(4, 1))
    own_f.wait()
    for dyh in (0, 1):
        for dx in range(NX):
            for h in range(2):
                f_await(dx, dyh, 1, h)

    def project(chunk, carry):
        total = dot(feat[chunk, 0], wbuf[0:4].reshape(DBLK, COLS))
        for j in range(1, 4):
            total = total + dot(feat[chunk, j], wbuf[4 * j : 4 * j + 4].reshape(DBLK, COLS))
        rounded = total.astype(BF16)
        signal = rounded[:, :LANES].astype(F32) * rounded[:, LANES : 2 * LANES].astype(F32)
        gmsg[chunk] = rounded[:, 2 * LANES :]
        turned = signal.T
        parts = [turned[:, i * N1 : (i + 1) * N1].reshape(Q, 1, CB, N1) for i in range(2)]
        stacked = jnp.concatenate(parts, 1).reshape(Q, 2 * CB, N1)
        sigmsg[:, pl.ds(pl.multiple_of(chunk * 16, 16), 16)] = stacked.astype(BF16)
        return carry

    lax.fori_loop(0, NX, project, 0)

    def s_copy(target, where):
        return pltpu.make_async_remote_copy(
            src_ref=sigmsg.at[target],
            dst_ref=xs.at[q],
            send_sem=bulk_send.at[1],
            recv_sem=bulk_recv.at[1],
            device_id=where,
            device_id_type=MESH,
        )

    def send_s(step, carry):
        target = lax.rem(q + step, Q)
        s_copy(target, {"y_lo": target // NZ, "z": lax.rem(target, NZ)}).start()
        return carry

    lax.fori_loop(1, Q, send_s, 0)
    own_s = pltpu.make_async_copy(sigmsg.at[q], xs.at[q], local_sem.at[3])
    own_s.start()

    gates = []
    for step in (1, 3, 2):
        copy = pltpu.make_async_remote_copy(
            src_ref=gmsg.at[wrap(x + step, NX)],
            dst_ref=gbuf.at[x],
            send_sem=g_send.at[step - 1],
            recv_sem=g_recv.at[3 - step],
            device_id=at_x(step),
            device_id_type=MESH,
        )
        copy.start()
        gates.append(copy)
    own_g = pltpu.make_async_copy(gmsg.at[x], gbuf.at[x], local_sem.at[4])
    own_g.start()

    def bulk_wait(index, src, dst):
        copy = pltpu.make_async_remote_copy(
            src_ref=src,
            dst_ref=dst,
            send_sem=bulk_send.at[index],
            recv_sem=bulk_recv.at[index],
            device_id=over_core,
            device_id_type=MESH,
        )
        copy.wait_send()
        copy.wait_recv()

    own_h.wait()
    bulk_wait(0, hmsg.at[pl.ds(0, NS - 1)], hbuf.at[:, pl.ds(0, (NS - 1) * 2 * CB)])
    hre[...] = hbuf[0].astype(F32)
    him[...] = hbuf[1].astype(F32)

    own_s.wait()
    bulk_wait(1, sigmsg.at[pl.ds(0, Q - 1)], xs.at[pl.ds(0, Q - 1)])
    xf[...] = xs[...].reshape(N1 * CB, N1).astype(F32)

    tc, ts = tc_ref[...], ts_ref[...]
    for c in range(CB):
        rows = pl.ds(c, N1, stride=CB)
        value = xf[rows, :].astype(BF16)
        step1 = dot(first_ref[...], jnp.concatenate([value, value], 0))
        re, im = step1[:N1], step1[N1:]
        turned = jnp.concatenate([re * tc + im * ts, im * tc - re * ts], 1)
        spectrum = three_pass(dot_nt, forward_ref[...], turned)
        re, im = spectrum[:N1], spectrum[N1:]
        fr, fi = hre[rows, :], him[rows, :]
        filtered = jnp.concatenate([fr * re - fi * im, fr * im + fi * re], 0)
        step3 = three_pass(dot, back_ref[...], filtered)
        re, im = step3[:N1], step3[N1:]
        turned = jnp.concatenate([re * tc - im * ts, im * tc + re * ts], 1)
        yf[rows, :] = three_pass(dot_nt, last_ref[...], turned)
    ybf[...] = yf[...].astype(BF16)

    def y_copy(s, where):
        return pltpu.make_async_remote_copy(
            src_ref=ybf.at[pl.ds(pl.multiple_of(s * 2 * CB, 2 * CB), 2 * CB)],
            dst_ref=ybuf.at[me_m],
            send_sem=bulk_send.at[2],
            recv_sem=bulk_recv.at[2],
            device_id=where,
            device_id_type=MESH,
        )

    def send_y(step, carry):
        _, s, where = peer(step)
        y_copy(s, where).start()
        return carry

    lax.fori_loop(1, NS, send_y, 0)
    own_y = pltpu.make_async_copy(ybf.at[own_rows], ybuf.at[me_m], local_sem.at[5])
    own_y.start()
    own_g.wait()
    for copy in gates:
        copy.wait()
    own_y.wait()
    bulk_wait(2, ybf.at[pl.ds(0, (NS - 1) * 2 * CB)], ybuf.at[pl.ds(0, NS - 1)])

    for chunk in range(NX):
        value = ybuf[chunk * Q : (chunk + 1) * Q].astype(F32)
        for i in range(2):
            block = value[:, i * CB : (i + 1) * CB].reshape(LANES, N1).T
            gate = gbuf[chunk, i * N1 : (i + 1) * N1, :].astype(F32)
            out_ref[i * N1 : (i + 1) * N1, chunk * LANES : (chunk + 1) * LANES] = (
                gate * block
            ).astype(BF16)

    for _, copy in started:
        copy.wait_send()


def shards(features, w_in, filter_real, filter_imag, skip_gain):
    d_rows, _, width = w_in.shape
    slices = w_in.reshape(d_rows, 3, NX, LANES).transpose(2, 0, 1, 3).reshape(NX, d_rows, COLS)
    consts = [jnp.asarray(table) for table in tables()]
    vmem = pl.BlockSpec(memory_space=pltpu.VMEM)
    hbm = pl.BlockSpec(memory_space=pl.ANY)
    dma = pltpu.SemaphoreType.DMA
    return pl.pallas_call(
        kernel,
        out_shape=jax.ShapeDtypeStruct((ROWS, width), BF16),
        in_specs=[hbm, hbm] + [vmem] * 9,
        out_specs=vmem,
        scratch_shapes=[
            pltpu.VMEM((NX, YH * NC, ROWS, DBLK), BF16),
            pltpu.VMEM((Q, WROWS, COLS), BF16),
            pltpu.VMEM((NS, 2, 2 * CB, N1), BF16),
            pltpu.VMEM((2, N1 * CB, N1), BF16),
            pltpu.VMEM((Q, 8 * CB, N1), BF16),
            pltpu.VMEM((Q, 8 * CB, N1), BF16),
            pltpu.VMEM((NX, ROWS, LANES), BF16),
            pltpu.VMEM((NX, ROWS, LANES), BF16),
            pltpu.VMEM((N1 * CB, N1), BF16),
            pltpu.VMEM((NS, 2 * CB, N1), BF16),
            pltpu.VMEM((N1 * CB, N1), F32),
            pltpu.VMEM((N1 * CB, N1), F32),
            pltpu.VMEM((N1 * CB, N1), F32),
            pltpu.VMEM((N1 * CB, N1), F32),
            dma((40,)),
            dma((32,)),
            dma((20,)),
            dma((3,)),
            dma((16,)),
            dma((3,)),
            dma((3,)),
            dma((3,)),
            dma((3,)),
            dma((6,)),
        ],
        compiler_params=pltpu.CompilerParams(
            collective_id=0, has_side_effects=True, vmem_limit_bytes=48 * 1024 * 1024
        ),
    )(features, slices, filter_real, filter_imag, skip_gain[None, :], *consts)


def solution(mesh):
    fine = Mesh(
        mesh.devices.reshape(YL, NZ, NX, YH, NC), ("y_lo", "z", "x", "y_hi", "core")
    )
    seq, chan = ("y_lo", "z", "x"), ("y_hi", "core")
    placed = (P(seq, chan), P(seq, None, chan), P(seq, chan), P(seq, chan), P(chan))
    return jax.shard_map(
        shards, mesh=fine, in_specs=placed, out_specs=P(seq, chan), check_vma=False
    )
```

time: 795 us -> 109 us (0.14); the launches traced: 783 us -> 108 us
  waiting for transfers between devices: 657 us -> 0 us
  Pallas kernels: 0 us -> 99.1 us
  starting transfers between devices: 52.8 us -> 0 us
  other arithmetic: 19.8 us -> 0 us
  local copies, waits for them, and re-layouts: 24.8 us -> 9.05 us
  matrix products: 14.7 us -> 0 us
  between operations: 13.7 us -> 0.06 us
    all_gather x2 -> x0, waiting for transfers between devices: 338 us -> none  [the longest x1 327 us: shards(): lax.all_gather(w_in, 'seq', axis=0, tiled=True)]
    ppermute x23 -> x0, waiting for transfers between devices: 314 us -> none  [swapped(): return lax.ppermute(block, axis, route)]
    pallas_call x0 -> x1, Pallas kernels: none -> 99.1 us  [shards(): pl.pallas_call(kernel, out_shape=jax.ShapeDtypeStruct((ROWS, width), BF16...]
    ppermute x23 -> x0, starting transfers between devices: 38.2 us -> none  [swapped(): return lax.ppermute(block, axis, route)]
    all_gather x1 -> x0, local copies, waits for them, and re-layouts: 17 us -> none  [shards(): lax.all_gather(w_in, 'seq', axis=0, tiled=True)]
    dot_general x3 -> x0, matrix products: 14.7 us -> none  [the longest x1 8.65 us: add_rows(): jnp.dot(gathered, panel.reshape(panel.shape[0], -1), preferred_element_ty...]
    all_to_all x2 -> x0, starting transfers between devices: 14.6 us -> none  [the longest x1 8.32 us: spread_filter(): lax.all_to_all(reorder(filter_real), 'seq', split_axis=1, concat_axis=0,...]
    select_n x6 -> x0, other arithmetic: 8.04 us -> none  [the longest x5 7.86 us: forward_butterfly(): jnp.where(upper_half, diff_re * cos_t - diff_im * sin_t, real_part + othe...]
  transfers between devices with their start and end apart: 27 -> 0, of which waited for: 26 -> 0; matrix products, arithmetic and copies ran while one was open for 4% -> 0% of each run, Pallas kernels for 0% -> 0%
where the time goes in v1:
time: 109 us; the launch traced here: 108 us
  Pallas kernels  99.1 us (91%)
  local copies, waits for them, and re-layouts  9.05 us (8%)
    pallas_call x1, Pallas kernels, shards(): pl.pallas_call(kernel, out_shape=jax.ShapeDtypeStruct((ROWS, width), BF16...  99.1 us
    unnamed x21, local copies, waits for them, and re-layouts  7.67 us

profile of v1, /device:TPU:8, one launch (start us, length us, event | category | flops | bytes accessed | tf_op | source)
XLA Modules:
  0.0 108.2 jit_solution(9585917825744648901)
XLA Ops:
  0.0 0.0 copy-start.1
  0.0 1.0 reshape.6
  1.0 0.0 copy-start
  1.1 0.2 copy.15
  1.2 0.0 copy-start.3
  1.2 0.2 reshape.7.w_ref
  1.4 0.0 copy-done.1
  1.4 0.7 copy-done
  2.1 0.1 copy-done.3
  2.2 0.0 copy-start.2
  2.2 1.0 copy-done.2
  3.3 0.0 copy-start.4
  3.3 0.9 copy-done.4
  4.2 0.0 copy-start.5
  4.2 0.9 copy-done.5
  5.1 0.0 copy-start.6
  5.1 0.9 copy-done.6
  6.0 0.0 copy-start.7
  6.0 0.8 copy-done.7
  6.9 0.0 copy-start.8
  6.9 0.8 copy-done.8
  7.7 0.0 copy-start.9
  7.7 0.7 copy-done.9
  8.4 99.1 %shard_map.109 = bf16[256,512]{1,0:T(8,128)(2,1)S(1)} custom-call(bf16[256,1024]{1,0:T(8,128)(2,1)S(1)} %copy-done, bf16[4,64,384]{2,1,0:T(8,128)(2,1)S(1)} %reshape.7.w_ref, f32[256,512]{1,0:T(8,128)S(1)} %copy-done.1, f32[256,512]{1,0:T(8,128)S(1)} %copy-done.2, f32[1,512]{1,0:T(1,128)S(1)} %bitcast.6, bf16[256,256]{1,0:T(8,128)(2,1)S(1)} %copy-done.6, ...), custom_call_target="tpu_custom_call" | custom-call | tf_op jit(solution)/shard_map/pallas_call | solution.py:457
  107.5 0.7 copy.17
Async XLA Ops:
  0.0 1.4 %copy-start.1 = (f32[256,512]{1,0:T(8,128)S(1)}, f32[256,512]{1,0:T(8,128)}, u32[]{:S(2)}) copy-start(f32[256,512]{1,0:T(8,128)} %fre_ref.1) | copy-start | bytes 1572868
  1.0 1.1 copy-start
  1.2 1.0 copy-start.3
  2.2 1.0 copy-start.2
  3.3 0.9 copy-start.4
  4.2 0.9 copy-start.5
  5.1 0.9 copy-start.6
  6.0 0.8 copy-start.7
  6.9 0.8 copy-start.8
  7.7 0.7 copy-start.9

commit v2 on v1

--- a/solution.py
+++ b/solution.py
@@ -47,14 +47,8 @@
     forward = np.concatenate(pair(np.block([[cos, sin], [-sin, cos]])), 0)
     back = np.concatenate(pair(np.block([[cos, -sin], [sin, cos]])), 0)
     last = np.concatenate(pair(np.concatenate([cos, -sin], 1) / (N1 * N1)), 0)
-    return (
-        first,
-        forward,
-        back,
-        last,
-        np.cos(twist).astype(np.float32),
-        np.sin(twist).astype(np.float32),
-    )
+    twist = np.stack([np.cos(twist), np.sin(twist)]).astype(np.float32)
+    return np.concatenate([first, forward, back, last], 0), twist
 
 
 def dot(a, b):
@@ -75,15 +69,11 @@
 def kernel(
     feat_ref,
     w_ref,
-    fre_ref,
-    fim_ref,
-    skip_ref,
-    first_ref,
-    forward_ref,
-    back_ref,
-    last_ref,
-    tc_ref,
-    ts_ref,
+    fre_hbm,
+    fim_hbm,
+    skip_hbm,
+    dft_hbm,
+    twist_hbm,
     out_ref,
     feat,
     wbuf,
@@ -99,6 +89,11 @@
     yf,
     hre,
     him,
+    fre_ref,
+    fim_ref,
+    skip_ref,
+    dft_ref,
+    twist_ref,
     f_send,
     f_recv,
     w_send,
@@ -109,6 +104,8 @@
     bulk_send,
     bulk_recv,
     local_sem,
+    in_sem,
+    own_w_sem,
 ):
     yl = lax.axis_index("y_lo")
     z = lax.axis_index("z")
@@ -135,17 +132,28 @@
         px, pq = m // Q, lax.rem(m, Q)
         return m, pq * NX + px, {"x": px, "y_lo": pq // NZ, "z": lax.rem(pq, NZ)}
 
+    fetches = [
+        pltpu.make_async_copy(src, dst, in_sem.at[index])
+        for index, (src, dst) in enumerate(
+            (
+                (fre_hbm, fre_ref),
+                (fim_hbm, fim_ref),
+                (skip_hbm, skip_ref),
+                (dft_hbm, dft_ref),
+                (twist_hbm, twist_ref),
+            )
+        )
+    ]
+    for fetch in fetches:
+        fetch.start()
+
     barrier = pltpu.get_barrier_semaphore()
 
-    def greet(step, carry):
-        _, _, where = peer(step)
+    for where in (at_x(1),at_x(2),at_x(-1),at_z(1),at_z(-1),over_yl):
         pl.semaphore_signal(barrier, inc=1, device_id=where, device_id_type=MESH)
-        return carry
-
-    lax.fori_loop(1, NS, greet, 0)
     pl.semaphore_signal(barrier, inc=1, device_id=over_yh, device_id_type=MESH)
     pl.semaphore_signal(barrier, inc=1, device_id=over_core, device_id_type=MESH)
-    pl.semaphore_wait(barrier, NS + 1)
+    pl.semaphore_wait(barrier, 8)
 
     started = []
 
@@ -175,13 +183,30 @@
             device_id_type=MESH,
         ).wait_recv()
 
-    def w_slot(dx):
-        return wbuf.at[q, pl.ds(pl.multiple_of(wrap(x + dx, NX) * 64, 64), 64)]
-
-    own_w = pltpu.make_async_copy(w_ref.at[x], w_slot(0), local_sem.at[0])
-    own_w.start()
+    def w_slot(dx, panel=None):
+        rows = pl.ds(pl.multiple_of(wrap(x + dx, NX) * 64, 64), 64)
+        if panel is None:
+            return wbuf.at[q, rows]
+        return wbuf.at[q, rows, pl.ds(panel * LANES, LANES)]
+
+    def w_panel(dx, panel):
+        lanes = pl.ds(pl.multiple_of(wrap(x + dx, NX) * LANES, LANES), LANES)
+        return w_ref.at[panel, :, lanes]
+
+    own_w = [
+        pltpu.make_async_copy(w_panel(0, panel), w_slot(0, panel), own_w_sem.at[panel])
+        for panel in range(3)
+    ]
+    for copy in own_w:
+        copy.start()
     for step in (1, 3, 2):
-        w_go(w_ref.at[wrap(x + step, NX)], w_slot(0), ws_recv.at[3 - step], at_x(step))
+        for panel in range(3):
+            w_go(
+                w_panel(step, panel),
+                w_slot(0, panel),
+                ws_recv.at[(3 - step) * 3 + panel],
+                at_x(step),
+            )
 
     def f_block(dx, dyh, dc, h):
         column = (yh if dyh == 0 else 1 - yh) * NC + (core if dc == 0 else 1 - core)
@@ -243,9 +268,11 @@
     def forward_w(dz, dyl):
         block = w_block(dz, dyl)
         if (dz, dyl) == (0, 0):
-            own_w.wait()
+            for copy in own_w:
+                copy.wait()
             for step in range(3):
-                w_await(w_slot(1 + step), ws_recv.at[step])
+                for panel in range(3):
+                    w_await(w_slot(1 + step, panel), ws_recv.at[step * 3 + panel])
             w_go(block, block, w_sem(0, 1), over_yl)
         else:
             w_await(block, w_sem(dz, dyl))
@@ -269,9 +296,9 @@
         filter_rows(1, fim_ref, chunk)
         return carry
 
-    forward_w(0, 0)
+    for fetch in fetches[:3]:
+        fetch.wait()
     lax.fori_loop(0, NX, filter_chunk, 0)
-    forward_w(0, 1)
     own_rows = pl.ds(pl.multiple_of(me_s * 2 * CB, 2 * CB), 2 * CB)
 
     def h_copy(m, where):
@@ -289,32 +316,38 @@
         h_copy(m, where).start()
         return carry
 
-    lax.fori_loop(1, NS, send_h, 0)
     own_h = pltpu.make_async_copy(hmsg.at[me_m], hbuf.at[:, own_rows], local_sem.at[2])
     own_h.start()
 
-    for dx in (3, 1):
-        forward_f(dx, 0, 0)
-    for dz in (-1, 1):
-        forward_w(dz, 0)
-    for dx in (3, 1):
-        forward_f(dx, 0, 1)
-    for dz in (-1, 1):
-        forward_w(dz, 1)
+    forward_w(0, 0)
+    forward_w(0, 1)
+    forward_f(3, 0, 0)
+    forward_f(1, 0, 0)
+    forward_w(-1, 0)
+    forward_w(1, 0)
     forward_f(0, 1, 0)
-    for dyl in (0, 1):
-        for dz in (-2, 2):
-            forward_w(dz, dyl)
+    forward_f(3, 0, 1)
+    forward_f(1, 0, 1)
+    forward_w(-1, 1)
+    forward_w(1, 1)
     forward_f(0, 1, 1)
-    for h in (0, 1):
-        for dx in (3, 1):
-            forward_f(dx, 1, h)
-    for dyl in (0, 1):
-        for dz in (-3, 3):
-            forward_w(dz, dyl)
-    for dyh in (0, 1):
-        for h in (0, 1):
-            forward_f(2, dyh, h)
+    forward_w(-2, 0)
+    forward_w(2, 0)
+    forward_f(3, 1, 0)
+    forward_f(1, 1, 0)
+    forward_w(-2, 1)
+    forward_w(2, 1)
+    forward_f(3, 1, 1)
+    forward_f(1, 1, 1)
+    forward_w(-3, 0)
+    forward_w(3, 0)
+    forward_w(-3, 1)
+    forward_w(3, 1)
+    forward_f(2, 0, 0)
+    forward_f(2, 0, 1)
+    forward_f(2, 1, 0)
+    forward_f(2, 1, 1)
+    lax.fori_loop(1, NS, send_h, 0)
     w_await(w_block(-4, 0), w_sem(-4, 0))
     w_await(w_block(4, 1), w_sem(4, 1))
     own_f.wait()
@@ -393,21 +426,25 @@
     bulk_wait(1, sigmsg.at[pl.ds(0, Q - 1)], xs.at[pl.ds(0, Q - 1)])
     xf[...] = xs[...].reshape(N1 * CB, N1).astype(F32)
 
-    tc, ts = tc_ref[...], ts_ref[...]
+    for fetch in fetches[3:]:
+        fetch.wait()
+    tc, ts = twist_ref[0], twist_ref[1]
+    first, last = dft_ref[0:256], dft_ref[1280:1536]
+    forward, back = dft_ref[256:768], dft_ref[768:1280]
     for c in range(CB):
         rows = pl.ds(c, N1, stride=CB)
         value = xf[rows, :].astype(BF16)
-        step1 = dot(first_ref[...], jnp.concatenate([value, value], 0))
+        step1 = dot(first, jnp.concatenate([value, value], 0))
         re, im = step1[:N1], step1[N1:]
         turned = jnp.concatenate([re * tc + im * ts, im * tc - re * ts], 1)
-        spectrum = three_pass(dot_nt, forward_ref[...], turned)
+        spectrum = three_pass(dot_nt, forward, turned)
         re, im = spectrum[:N1], spectrum[N1:]
         fr, fi = hre[rows, :], him[rows, :]
         filtered = jnp.concatenate([fr * re - fi * im, fr * im + fi * re], 0)
-        step3 = three_pass(dot, back_ref[...], filtered)
+        step3 = three_pass(dot, back, filtered)
         re, im = step3[:N1], step3[N1:]
         turned = jnp.concatenate([re * tc - im * ts, im * tc + re * ts], 1)
-        yf[rows, :] = three_pass(dot_nt, last_ref[...], turned)
+        yf[rows, :] = three_pass(dot_nt, last, turned)
     ybf[...] = yf[...].astype(BF16)
 
     def y_copy(s, where):
@@ -449,15 +486,15 @@
 
 def shards(features, w_in, filter_real, filter_imag, skip_gain):
     d_rows, _, width = w_in.shape
-    slices = w_in.reshape(d_rows, 3, NX, LANES).transpose(2, 0, 1, 3).reshape(NX, d_rows, COLS)
+    panels = w_in.transpose(1, 0, 2)
     consts = [jnp.asarray(table) for table in tables()]
     vmem = pl.BlockSpec(memory_space=pltpu.VMEM)
-    hbm = pl.BlockSpec(memory_space=pl.ANY)
+    hbm = pl.BlockSpec(memory_space=pltpu.HBM)
     dma = pltpu.SemaphoreType.DMA
     return pl.pallas_call(
         kernel,
         out_shape=jax.ShapeDtypeStruct((ROWS, width), BF16),
-        in_specs=[hbm, hbm] + [vmem] * 9,
+        in_specs=[hbm] * 7,
         out_specs=vmem,
         scratch_shapes=[
             pltpu.VMEM((NX, YH * NC, ROWS, DBLK), BF16),
@@ -474,21 +511,28 @@
             pltpu.VMEM((N1 * CB, N1), F32),
             pltpu.VMEM((N1 * CB, N1), F32),
             pltpu.VMEM((N1 * CB, N1), F32),
+            pltpu.VMEM((ROWS, width), F32),
+            pltpu.VMEM((ROWS, width), F32),
+            pltpu.VMEM((1, width), F32),
+            pltpu.VMEM((1536, 256), BF16),
+            pltpu.VMEM((2, N1, N1), F32),
             dma((40,)),
             dma((32,)),
-            dma((20,)),
-            dma((3,)),
+            dma((32,)),
+            dma((9,)),
             dma((16,)),
             dma((3,)),
             dma((3,)),
             dma((3,)),
             dma((3,)),
             dma((6,)),
+            dma((5,)),
+            dma((3,)),
         ],
         compiler_params=pltpu.CompilerParams(
-            collective_id=0, has_side_effects=True, vmem_limit_bytes=48 * 1024 * 1024
+            collective_id=0, has_side_effects=True, vmem_limit_bytes=56 * 1024 * 1024
         ),
-    )(features, slices, filter_real, filter_imag, skip_gain[None, :], *consts)
+    )(features, panels, filter_real, filter_imag, skip_gain[None, :], *consts)
 
 
 def solution(mesh):

time: 109 us -> 89.3 us (0.82)
  Pallas kernels: 99.1 us -> 87.5 us
  local copies, waits for them, and re-layouts: 9.05 us -> 1.67 us
    pallas_call x1, Pallas kernels: 99.1 us -> 87.5 us  [shards(): pl.pallas_call(kernel, out_shape=jax.ShapeDtypeStruct((ROWS, width), BF16...]
    unnamed x21 -> x1, local copies, waits for them, and re-layouts: 7.67 us -> 1.67 us
    reshape x3 -> x0, local copies, waits for them, and re-layouts: 1.38 us -> none  [shards(): w_in.reshape(d_rows, 3, NX, LANES).transpose(2, 0, 1, 3)]
where the time goes in v2:
time: 89.3 us; the launch traced here: 89.2 us
  Pallas kernels  87.5 us (98%)
  local copies, waits for them, and re-layouts  1.67 us (2%)
    pallas_call x1, Pallas kernels, shards(): pl.pallas_call(kernel, out_shape=jax.ShapeDtypeStruct((ROWS, width), BF16...  87.5 us

profile of v2, /device:TPU:8, one launch (start us, length us, event | category | flops | bytes accessed | tf_op | source)
XLA Modules:
  0.0 89.2 jit_solution(16635541090988523094)
XLA Ops:
  0.0 87.5 %shard_map.73 = bf16[256,512]{1,0:T(8,128)(2,1)} custom-call(bf16[256,1024]{1,0:T(8,128)(2,1)} %feat_ref.1, bf16[3,64,512]{2,1,0:T(8,128)(2,1)} %bitcast.2, f32[256,512]{1,0:T(8,128)} %fre_hbm.1, f32[256,512]{1,0:T(8,128)} %fim_hbm.1, f32[1,512]{1,0:T(1,128)} %bitcast.3, bf16[1536,256]{1,0:T(8,128)(2,1)} %constant.4.clone.dft_hbm, ...), custom_call_target="tpu_custom_call" | custom-call | tf_op jit(solution)/shard_map/pallas_call | solution.py:494
  87.5 1.7 %copy.9 = bf16[256,512]{1,0:T(8,128)(2,1)} copy(bf16[256,512]{1,0:T(8,128)(2,1)} %shard_map.73) | data formatting | bytes 524288

commit v3 on v2

--- a/solution.py
+++ b/solution.py
@@ -17,13 +17,117 @@
 NS = YL * NZ * NX
 Q = YL * NZ
 ROWS = 256
-HALF = ROWS // 2
+FPARTS = 4
+FROWS = ROWS // FPARTS
 DBLK = 1024
 LANES = 128
+GROUP = 8
 CB = 8
 N1 = 128
 WROWS = 64 * NX
 COLS = 3 * LANES
+
+
+PLAN = (
+    ("W", 0, 0, 0),
+    ("F", 0, 0, 0),
+    ("F", 0, 0, 1),
+    ("F", 0, 0, 2),
+    ("F", 0, 0, 3),
+    ("W", 0, 0, 1),
+    ("W", 0, 0, 3),
+    ("W", -1, 0, 0),
+    ("W", 1, 0, 0),
+    ("W", 0, 0, 2),
+    ("W", 0, 1, 0),
+    ("F", 1, 0, 0),
+    ("W", -1, 0, 1),
+    ("W", 1, 0, 1),
+    ("F", 3, 0, 0),
+    ("h", 0, 0, 0),
+    ("F", 0, 1, 0),
+    ("W", -1, 0, 3),
+    ("W", 1, 0, 3),
+    ("W", -2, 0, 0),
+    ("W", 2, 0, 0),
+    ("F", 1, 0, 1),
+    ("F", 3, 0, 1),
+    ("W", -1, 0, 2),
+    ("F", 0, 1, 1),
+    ("W", 1, 0, 2),
+    ("W", -1, 1, 0),
+    ("W", 1, 1, 0),
+    ("W", -2, 0, 1),
+    ("W", 2, 0, 1),
+    ("F", 1, 0, 2),
+    ("F", 3, 0, 2),
+    ("F", 0, 1, 2),
+    ("W", -2, 0, 3),
+    ("W", 2, 0, 3),
+    ("W", -3, 0, 0),
+    ("W", 3, 0, 0),
+    ("F", 1, 0, 3),
+    ("W", -2, 0, 2),
+    ("W", 2, 0, 2),
+    ("F", 3, 0, 3),
+    ("F", 0, 1, 3),
+    ("W", -2, 1, 0),
+    ("W", 2, 1, 0),
+    ("W", 0, 1, 1),
+    ("W", -3, 0, 1),
+    ("W", 3, 0, 1),
+    ("W", 0, 1, 3),
+    ("F", 1, 1, 0),
+    ("F", 2, 0, 0),
+    ("W", -3, 0, 3),
+    ("W", 3, 0, 3),
+    ("W", 0, 1, 2),
+    ("W", -4, 0, 0),
+    ("W", 3, 0, 2),
+    ("W", -3, 0, 2),
+    ("W", 3, 1, 0),
+    ("F", 2, 0, 1),
+    ("F", 3, 1, 0),
+    ("W", -3, 1, 0),
+    ("W", 1, 1, 1),
+    ("W", -1, 1, 1),
+    ("W", 1, 1, 3),
+    ("F", 1, 1, 1),
+    ("W", -4, 0, 1),
+    ("W", 1, 1, 2),
+    ("F", 3, 1, 1),
+    ("W", -1, 1, 3),
+    ("W", -4, 1, 0),
+    ("W", -4, 0, 3),
+    ("W", 2, 1, 1),
+    ("F", 2, 1, 1),
+    ("F", 1, 1, 2),
+    ("F", 2, 0, 2),
+    ("W", -1, 1, 2),
+    ("W", 2, 1, 3),
+    ("W", -4, 0, 2),
+    ("W", 2, 1, 2),
+    ("W", -2, 1, 1),
+    ("W", 3, 1, 1),
+    ("F", 2, 0, 3),
+    ("F", 3, 1, 2),
+    ("W", -2, 1, 3),
+    ("W", 3, 1, 3),
+    ("W", -2, 1, 2),
+    ("W", 3, 1, 2),
+    ("F", 1, 1, 3),
+    ("W", -3, 1, 1),
+    ("F", 3, 1, 3),
+    ("W", -4, 1, 1),
+    ("W", -3, 1, 3),
+    ("W", -4, 1, 3),
+    ("W", -3, 1, 2),
+    ("F", 2, 1, 3),
+    ("W", -4, 1, 2),
+    ("F", 2, 1, 2),
+    ("F", 2, 1, 0),
+    ("H", 0, 1, 0),
+)
 
 
 def split16(table):
@@ -155,25 +259,24 @@
     pl.semaphore_signal(barrier, inc=1, device_id=over_core, device_id_type=MESH)
     pl.semaphore_wait(barrier, 8)
 
-    started = []
-
-    def w_block(dz, dyl):
-        return wbuf.at[(yl if dyl == 0 else 1 - yl) * NZ + wrap(z + dz, NZ)]
-
-    def w_go(src, dst, recv_sem, where):
-        index = len([1 for kind, _ in started if kind == "w"])
+    own_f = pltpu.make_async_copy(feat_ref, feat.at[x, yh * NC + core], local_sem.at[1])
+    own_f.start()
+
+    w_started, f_started = [], []
+
+    def go(started, sems, src, dst, recv_sem, where):
         copy = pltpu.make_async_remote_copy(
             src_ref=src,
             dst_ref=dst,
-            send_sem=w_send.at[index],
+            send_sem=sems.at[len(started)],
             recv_sem=recv_sem,
             device_id=where,
             device_id_type=MESH,
         )
         copy.start()
-        started.append(("w", copy))
-
-    def w_await(dst, recv_sem):
+        started.append(copy)
+
+    def arrived(dst, recv_sem):
         pltpu.make_async_remote_copy(
             src_ref=dst,
             dst_ref=dst,
@@ -183,103 +286,87 @@
             device_id_type=MESH,
         ).wait_recv()
 
-    def w_slot(dx, panel=None):
+    def w_piece(dz, dyl, dx, panel=None):
+        place = (yl if dyl == 0 else 1 - yl) * NZ + wrap(z + dz, NZ)
         rows = pl.ds(pl.multiple_of(wrap(x + dx, NX) * 64, 64), 64)
         if panel is None:
-            return wbuf.at[q, rows]
-        return wbuf.at[q, rows, pl.ds(panel * LANES, LANES)]
+            return wbuf.at[place, rows]
+        return wbuf.at[place, rows, pl.ds(panel * LANES, LANES)]
 
     def w_panel(dx, panel):
         lanes = pl.ds(pl.multiple_of(wrap(x + dx, NX) * LANES, LANES), LANES)
         return w_ref.at[panel, :, lanes]
 
+    def w_go(here, there, where):
+        dz, dyl, dx = there
+        piece = w_piece(*here)
+        recv_sem = w_recv.at[(dz % NZ * 2 + dyl) * NX + dx]
+        go(w_started, w_send, piece, piece, recv_sem, where)
+
+    def weights_arrived(dz, dyl, dx):
+        here = (dz, dyl, dx)
+        if here == (0, 0, 0):
+            for copy in own_w:
+                copy.wait()
+        elif here[:2] == (0, 0):
+            for panel in range(3):
+                arrived(w_piece(0, 0, dx, panel), ws_recv.at[(dx - 1) * 3 + panel])
+        else:
+            arrived(w_piece(*here), w_recv.at[(dz % NZ * 2 + dyl) * NX + dx])
+        if -3 < dz <= 0 or (dz == -3 and dyl == 0):
+            w_go(here, (dz - 1, dyl, dx), at_z(1))
+        if 0 <= dz < 3 or (dz == 3 and dyl == 1):
+            w_go(here, (dz + 1, dyl, dx), at_z(-1))
+        if here[:2] == (0, 0):
+            w_go(here, (0, 1, dx), over_yl)
+
     own_w = [
-        pltpu.make_async_copy(w_panel(0, panel), w_slot(0, panel), own_w_sem.at[panel])
+        pltpu.make_async_copy(w_panel(0, panel), w_piece(0, 0, 0, panel), own_w_sem.at[panel])
         for panel in range(3)
     ]
     for copy in own_w:
         copy.start()
     for step in (1, 3, 2):
         for panel in range(3):
-            w_go(
+            go(
+                w_started,
+                w_send,
                 w_panel(step, panel),
-                w_slot(0, panel),
+                w_piece(0, 0, 0, panel),
                 ws_recv.at[(3 - step) * 3 + panel],
                 at_x(step),
             )
 
-    def f_block(dx, dyh, dc, h):
+    def f_piece(dx, dyh, dc, h):
         column = (yh if dyh == 0 else 1 - yh) * NC + (core if dc == 0 else 1 - core)
-        return feat.at[wrap(x + dx, NX), column, pl.ds(h * HALF, HALF)]
+        return feat.at[wrap(x + dx, NX), column, pl.ds(h * FROWS, FROWS)]
 
     def f_sem(dx, dyh, dc, h):
-        return f_recv.at[((dx % NX * 2 + dyh) * 2 + dc) * 2 + h]
-
-    def f_go(src, block, here, where):
-        dx, dyh, dc, h = here
-        index = len([1 for kind, _ in started if kind == "f"])
-        copy = pltpu.make_async_remote_copy(
-            src_ref=src,
-            dst_ref=block,
-            send_sem=f_send.at[index],
-            recv_sem=f_sem(dx, dyh, dc, h),
-            device_id=where,
-            device_id_type=MESH,
-        )
-        copy.start()
-        started.append(("f", copy))
-
-    def f_await(dx, dyh, dc, h):
-        block = f_block(dx, dyh, dc, h)
-        pltpu.make_async_remote_copy(
-            src_ref=block,
-            dst_ref=block,
-            send_sem=f_send.at[0],
-            recv_sem=f_sem(dx, dyh, dc, h),
-            device_id=over_core,
-            device_id_type=MESH,
-        ).wait_recv()
-
-    for h in range(2):
-        src = feat_ref.at[pl.ds(h * HALF, HALF)]
-        block = f_block(0, 0, 0, h)
-        f_go(src, block, (3, 0, 0, h), at_x(1))
-        f_go(src, block, (1, 0, 0, h), at_x(-1))
-        f_go(src, block, (0, 1, 0, h), over_yh)
-        f_go(src, block, (0, 0, 1, h), over_core)
-    own_f = pltpu.make_async_copy(feat_ref, feat.at[x, yh * NC + core], local_sem.at[1])
-    own_f.start()
-
-    def forward_f(dx, dyh, h):
-        f_await(dx, dyh, 0, h)
-        block = f_block(dx, dyh, 0, h)
+        return f_recv.at[((dx % NX * 2 + dyh) * 2 + dc) * FPARTS + h]
+
+    def features_arrived(dx, dyh, h):
+        piece = f_piece(dx, dyh, 0, h)
+        src = piece
+        if (dx, dyh) == (0, 0):
+            src = feat_ref.at[pl.ds(h * FROWS, FROWS)]
+        else:
+            arrived(piece, f_sem(dx, dyh, 0, h))
+
+        def pass_on(there, where):
+            go(f_started, f_send, src, piece, f_sem(*there), where)
+
         if dx == 0:
-            f_go(block, block, (3, dyh, 0, h), at_x(1))
-            f_go(block, block, (1, dyh, 0, h), at_x(-1))
-        if dx == 3 and h == 0:
-            f_go(block, block, (2, dyh, 0, h), at_x(1))
-        if dx == 1 and h == 1:
-            f_go(block, block, (2, dyh, 0, h), at_x(-1))
-        f_go(block, block, (dx, dyh, 1, h), over_core)
-
-    def w_sem(dz, dyl):
-        return w_recv.at[dz % NZ * 2 + dyl]
-
-    def forward_w(dz, dyl):
-        block = w_block(dz, dyl)
-        if (dz, dyl) == (0, 0):
-            for copy in own_w:
-                copy.wait()
-            for step in range(3):
-                for panel in range(3):
-                    w_await(w_slot(1 + step, panel), ws_recv.at[step * 3 + panel])
-            w_go(block, block, w_sem(0, 1), over_yl)
-        else:
-            w_await(block, w_sem(dz, dyl))
-        if -3 < dz <= 0 or (dz == -3 and dyl == 0):
-            w_go(block, block, w_sem(dz - 1, dyl), at_z(1))
-        if 0 <= dz < 3 or (dz == 3 and dyl == 1):
-            w_go(block, block, w_sem(dz + 1, dyl), at_z(-1))
+            pass_on((3, dyh, 0, h), at_x(1))
+            pass_on((1, dyh, 0, h), at_x(-1))
+        if (dx, dyh) == (0, 0):
+            pass_on((0, 1, 0, h), over_yh)
+        elif (dx, dyh) == (2, 0) and h % 2 == 1:
+            pass_on((2, 1, 0, h), over_yh)
+        elif dx in (1, 3):
+            turn = (3, 1, 3, 1) if dyh == 0 else (3, 0, 1, 0)
+            if turn[h] == dx:
+                pass_on((2, dyh, 0, h), at_x(1 if dx == 3 else -1))
+        pass_on((dx, dyh, 1, h), over_core)
 
     def filter_rows(part, ref, chunk):
         lanes = pl.ds(pl.multiple_of(chunk * LANES, LANES), LANES)
@@ -296,9 +383,6 @@
         filter_rows(1, fim_ref, chunk)
         return carry
 
-    for fetch in fetches[:3]:
-        fetch.wait()
-    lax.fori_loop(0, NX, filter_chunk, 0)
     own_rows = pl.ds(pl.multiple_of(me_s * 2 * CB, 2 * CB), 2 * CB)
 
     def h_copy(m, where):
@@ -317,44 +401,24 @@
         return carry
 
     own_h = pltpu.make_async_copy(hmsg.at[me_m], hbuf.at[:, own_rows], local_sem.at[2])
-    own_h.start()
-
-    forward_w(0, 0)
-    forward_w(0, 1)
-    forward_f(3, 0, 0)
-    forward_f(1, 0, 0)
-    forward_w(-1, 0)
-    forward_w(1, 0)
-    forward_f(0, 1, 0)
-    forward_f(3, 0, 1)
-    forward_f(1, 0, 1)
-    forward_w(-1, 1)
-    forward_w(1, 1)
-    forward_f(0, 1, 1)
-    forward_w(-2, 0)
-    forward_w(2, 0)
-    forward_f(3, 1, 0)
-    forward_f(1, 1, 0)
-    forward_w(-2, 1)
-    forward_w(2, 1)
-    forward_f(3, 1, 1)
-    forward_f(1, 1, 1)
-    forward_w(-3, 0)
-    forward_w(3, 0)
-    forward_w(-3, 1)
-    forward_w(3, 1)
-    forward_f(2, 0, 0)
-    forward_f(2, 0, 1)
-    forward_f(2, 1, 0)
-    forward_f(2, 1, 1)
-    lax.fori_loop(1, NS, send_h, 0)
-    w_await(w_block(-4, 0), w_sem(-4, 0))
-    w_await(w_block(4, 1), w_sem(4, 1))
+    for kind, one, two, three in PLAN:
+        if kind == "W":
+            weights_arrived(one, two, three)
+        elif kind == "F":
+            features_arrived(one, two, three)
+        elif kind == "h":
+            for fetch in fetches[:3]:
+                fetch.wait()
+            lax.fori_loop(0, NX, filter_chunk, 0)
+            own_h.start()
+        elif kind == "H":
+            share = NS // two
+            lax.fori_loop(max(1, one * share), (one + 1) * share, send_h, 0)
     own_f.wait()
-    for dyh in (0, 1):
-        for dx in range(NX):
-            for h in range(2):
-                f_await(dx, dyh, 1, h)
+    for dx in range(NX):
+        for dyh in (0, 1):
+            for h in range(FPARTS):
+                arrived(f_piece(dx, dyh, 1, h), f_sem(dx, dyh, 1, h))
 
     def project(chunk, carry):
         total = dot(feat[chunk, 0], wbuf[0:4].reshape(DBLK, COLS))
@@ -428,23 +492,44 @@
 
     for fetch in fetches[3:]:
         fetch.wait()
-    tc, ts = twist_ref[0], twist_ref[1]
+    wide = GROUP * N1
+
+    def tiled(table):
+        return jnp.concatenate([table] * GROUP, 1)
+
+    tc, ts = tiled(twist_ref[0]), tiled(twist_ref[1])
     first, last = dft_ref[0:256], dft_ref[1280:1536]
     forward, back = dft_ref[256:768], dft_ref[768:1280]
-    for c in range(CB):
-        rows = pl.ds(c, N1, stride=CB)
-        value = xf[rows, :].astype(BF16)
+
+    def stack(re, im):
+        return jnp.concatenate(
+            [
+                jnp.concatenate([t[:, g * N1 : (g + 1) * N1] for g in range(GROUP)], 0)
+                for t in (re, im)
+            ],
+            1,
+        )
+
+    for base in range(0, CB, GROUP):
+        rows = [pl.ds(base + g, N1, stride=CB) for g in range(GROUP)]
+
+        def lanes(ref):
+            return jnp.concatenate([ref[r, :] for r in rows], 1)
+
+        value = lanes(xf).astype(BF16)
         step1 = dot(first, jnp.concatenate([value, value], 0))
         re, im = step1[:N1], step1[N1:]
-        turned = jnp.concatenate([re * tc + im * ts, im * tc - re * ts], 1)
+        turned = stack(re * tc + im * ts, im * tc - re * ts)
         spectrum = three_pass(dot_nt, forward, turned)
         re, im = spectrum[:N1], spectrum[N1:]
-        fr, fi = hre[rows, :], him[rows, :]
+        fr, fi = lanes(hre), lanes(him)
         filtered = jnp.concatenate([fr * re - fi * im, fr * im + fi * re], 0)
         step3 = three_pass(dot, back, filtered)
         re, im = step3[:N1], step3[N1:]
-        turned = jnp.concatenate([re * tc - im * ts, im * tc + re * ts], 1)
-        yf[rows, :] = three_pass(dot_nt, last, turned)
+        turned = stack(re * tc - im * ts, im * tc + re * ts)
+        result = three_pass(dot_nt, last, turned)
+        for g in range(GROUP):
+            yf[rows[g], :] = result[:, g * N1 : (g + 1) * N1]
     ybf[...] = yf[...].astype(BF16)
 
     def y_copy(s, where):
@@ -480,7 +565,7 @@
                 gate * block
             ).astype(BF16)
 
-    for _, copy in started:
+    for copy in w_started + f_started:
         copy.wait_send()
 
 
@@ -516,11 +601,11 @@
             pltpu.VMEM((1, width), F32),
             pltpu.VMEM((1536, 256), BF16),
             pltpu.VMEM((2, N1, N1), F32),
-            dma((40,)),
-            dma((32,)),
-            dma((32,)),
+            dma((80,)),
+            dma((16 * FPARTS,)),
+            dma((80,)),
             dma((9,)),
-            dma((16,)),
+            dma((64,)),
             dma((3,)),
             dma((3,)),
             dma((3,)),

time: 89.3 us -> 77.7 us (0.87)
  Pallas kernels: 87.5 us -> 75.8 us
    pallas_call x1, Pallas kernels: 87.5 us -> 75.8 us  [shards(): pl.pallas_call(kernel, out_shape=jax.ShapeDtypeStruct((ROWS, width), BF16...]
where the time goes in v3:
time: 77.7 us; the launch traced here: 77.5 us
  Pallas kernels  75.8 us (98%)
  local copies, waits for them, and re-layouts  1.67 us (2%)
    pallas_call x1, Pallas kernels, shards(): pl.pallas_call(kernel, out_shape=jax.ShapeDtypeStruct((ROWS, width), BF16...  75.8 us
    unnamed x1, local copies, waits for them, and re-layouts  1.67 us

profile of v3, /device:TPU:8, one launch (start us, length us, event | category | flops | bytes accessed | tf_op | source)
XLA Modules:
  0.0 77.5 jit_solution(13587086996090962462)
XLA Ops:
  0.0 75.8 %shard_map.73 = bf16[256,512]{1,0:T(8,128)(2,1)} custom-call(bf16[256,1024]{1,0:T(8,128)(2,1)} %feat_ref.1, bf16[3,64,512]{2,1,0:T(8,128)(2,1)} %bitcast.2, f32[256,512]{1,0:T(8,128)} %fre_hbm.1, f32[256,512]{1,0:T(8,128)} %fim_hbm.1, f32[1,512]{1,0:T(1,128)} %bitcast.3, bf16[1536,256]{1,0:T(8,128)(2,1)} %constant.4.clone.dft_hbm, ...), custom_call_target="tpu_custom_call" | custom-call | tf_op jit(solution)/shard_map/pallas_call | solution.py:579
  75.8 1.7 %copy.9 = bf16[256,512]{1,0:T(8,128)(2,1)} copy(bf16[256,512]{1,0:T(8,128)(2,1)} %shard_map.73) | data formatting | bytes 524288

commit v4 on v3

--- a/solution.py
+++ b/solution.py
@@ -31,23 +31,27 @@
 PLAN = (
     ("W", 0, 0, 0),
     ("F", 0, 0, 0),
+    ("Y", 0, 0, 0),
     ("F", 0, 0, 1),
     ("F", 0, 0, 2),
     ("F", 0, 0, 3),
+    ("Y", 1, 0, 0),
     ("W", 0, 0, 1),
     ("W", 0, 0, 3),
     ("W", -1, 0, 0),
     ("W", 1, 0, 0),
     ("W", 0, 0, 2),
     ("W", 0, 1, 0),
+    ("Y", 2, 0, 0),
     ("F", 1, 0, 0),
+    ("h", 0, 0, 0),
     ("W", -1, 0, 1),
     ("W", 1, 0, 1),
     ("F", 3, 0, 0),
-    ("h", 0, 0, 0),
     ("F", 0, 1, 0),
     ("W", -1, 0, 3),
     ("W", 1, 0, 3),
+    ("Y", 3, 0, 0),
     ("W", -2, 0, 0),
     ("W", 2, 0, 0),
     ("F", 1, 0, 1),
@@ -56,13 +60,15 @@
     ("F", 0, 1, 1),
     ("W", 1, 0, 2),
     ("W", -1, 1, 0),
+    ("W", 0, 1, 1),
     ("W", 1, 1, 0),
     ("W", -2, 0, 1),
+    ("W", 0, 1, 3),
     ("W", 2, 0, 1),
     ("F", 1, 0, 2),
     ("F", 3, 0, 2),
-    ("F", 0, 1, 2),
     ("W", -2, 0, 3),
+    ("W", 0, 1, 2),
     ("W", 2, 0, 3),
     ("W", -3, 0, 0),
     ("W", 3, 0, 0),
@@ -70,63 +76,67 @@
     ("W", -2, 0, 2),
     ("W", 2, 0, 2),
     ("F", 3, 0, 3),
-    ("F", 0, 1, 3),
+    ("F", 0, 1, 2),
     ("W", -2, 1, 0),
+    ("W", 1, 1, 1),
+    ("W", -1, 1, 1),
     ("W", 2, 1, 0),
-    ("W", 0, 1, 1),
-    ("W", -3, 0, 1),
-    ("W", 3, 0, 1),
-    ("W", 0, 1, 3),
     ("F", 1, 1, 0),
     ("F", 2, 0, 0),
+    ("W", -3, 0, 1),
+    ("W", 1, 1, 3),
+    ("F", 0, 1, 3),
+    ("W", -1, 1, 3),
+    ("W", 3, 0, 1),
     ("W", -3, 0, 3),
+    ("W", 1, 1, 2),
+    ("F", 2, 0, 1),
+    ("F", 3, 1, 0),
+    ("W", -1, 1, 2),
+    ("P", 0, (0, -1, 1), 1),
     ("W", 3, 0, 3),
-    ("W", 0, 1, 2),
     ("W", -4, 0, 0),
     ("W", 3, 0, 2),
+    ("F", 2, 1, 0),
+    ("F", 1, 1, 1),
     ("W", -3, 0, 2),
+    ("W", 2, 1, 1),
+    ("F", 3, 1, 1),
+    ("W", -3, 1, 0),
     ("W", 3, 1, 0),
-    ("F", 2, 0, 1),
-    ("F", 3, 1, 0),
-    ("W", -3, 1, 0),
-    ("W", 1, 1, 1),
-    ("W", -1, 1, 1),
-    ("W", 1, 1, 3),
-    ("F", 1, 1, 1),
+    ("W", -2, 1, 1),
+    ("W", 2, 1, 3),
+    ("F", 2, 1, 1),
+    ("F", 2, 0, 3),
+    ("F", 2, 0, 2),
     ("W", -4, 0, 1),
-    ("W", 1, 1, 2),
-    ("F", 3, 1, 1),
-    ("W", -1, 1, 3),
+    ("W", 2, 1, 2),
+    ("W", -2, 1, 3),
+    ("W", 3, 1, 1),
+    ("W", -4, 0, 3),
     ("W", -4, 1, 0),
-    ("W", -4, 0, 3),
-    ("W", 2, 1, 1),
-    ("F", 2, 1, 1),
     ("F", 1, 1, 2),
-    ("F", 2, 0, 2),
-    ("W", -1, 1, 2),
-    ("W", 2, 1, 3),
+    ("F", 3, 1, 2),
+    ("W", -2, 1, 2),
+    ("P", 0, (-2, 2), 0),
+    ("W", 3, 1, 3),
     ("W", -4, 0, 2),
-    ("W", 2, 1, 2),
-    ("W", -2, 1, 1),
-    ("W", 3, 1, 1),
-    ("F", 2, 0, 3),
-    ("F", 3, 1, 2),
-    ("W", -2, 1, 3),
-    ("W", 3, 1, 3),
-    ("W", -2, 1, 2),
     ("W", 3, 1, 2),
+    ("F", 2, 1, 3),
     ("F", 1, 1, 3),
     ("W", -3, 1, 1),
+    ("W", -4, 1, 1),
     ("F", 3, 1, 3),
-    ("W", -4, 1, 1),
+    ("H", 0, 1, 0),
     ("W", -3, 1, 3),
     ("W", -4, 1, 3),
     ("W", -3, 1, 2),
-    ("F", 2, 1, 3),
+    ("F", 2, 1, 2),
     ("W", -4, 1, 2),
-    ("F", 2, 1, 2),
-    ("F", 2, 1, 0),
-    ("H", 0, 1, 0),
+    ("P", 0, (-3, 3, -4), 2),
+    ("P", 1, (0, -1, 1, -2, 2, -3, 3, -4), 3),
+    ("P", 3, (0, -1, 1, -2, 2, -3, 3, -4), 3),
+    ("P", 2, (0, -1, 1, -2, 2, -3, 3, -4), 3),
 )
 
 
@@ -193,6 +203,7 @@
     yf,
     hre,
     him,
+    acc,
     fre_ref,
     fim_ref,
     skip_ref,
@@ -251,6 +262,26 @@
     for fetch in fetches:
         fetch.start()
 
+    def w_piece(dz, dyl, dx, panel=None):
+        place = (yl if dyl == 0 else 1 - yl) * NZ + wrap(z + dz, NZ)
+        rows = pl.ds(pl.multiple_of(wrap(x + dx, NX) * 64, 64), 64)
+        if panel is None:
+            return wbuf.at[place, rows]
+        return wbuf.at[place, rows, pl.ds(panel * LANES, LANES)]
+
+    def w_panel(dx, panel):
+        lanes = pl.ds(pl.multiple_of(wrap(x + dx, NX) * LANES, LANES), LANES)
+        return w_ref.at[panel, :, lanes]
+
+    own_w = [
+        pltpu.make_async_copy(w_panel(0, panel), w_piece(0, 0, 0, panel), own_w_sem.at[panel])
+        for panel in range(3)
+    ]
+    for copy in own_w:
+        copy.start()
+    own_f = pltpu.make_async_copy(feat_ref, feat.at[x, yh * NC + core], local_sem.at[1])
+    own_f.start()
+
     barrier = pltpu.get_barrier_semaphore()
 
     for where in (at_x(1),at_x(2),at_x(-1),at_z(1),at_z(-1),over_yl):
@@ -258,9 +289,6 @@
     pl.semaphore_signal(barrier, inc=1, device_id=over_yh, device_id_type=MESH)
     pl.semaphore_signal(barrier, inc=1, device_id=over_core, device_id_type=MESH)
     pl.semaphore_wait(barrier, 8)
-
-    own_f = pltpu.make_async_copy(feat_ref, feat.at[x, yh * NC + core], local_sem.at[1])
-    own_f.start()
 
     w_started, f_started = [], []
 
@@ -285,17 +313,6 @@
             device_id=over_core,
             device_id_type=MESH,
         ).wait_recv()
-
-    def w_piece(dz, dyl, dx, panel=None):
-        place = (yl if dyl == 0 else 1 - yl) * NZ + wrap(z + dz, NZ)
-        rows = pl.ds(pl.multiple_of(wrap(x + dx, NX) * 64, 64), 64)
-        if panel is None:
-            return wbuf.at[place, rows]
-        return wbuf.at[place, rows, pl.ds(panel * LANES, LANES)]
-
-    def w_panel(dx, panel):
-        lanes = pl.ds(pl.multiple_of(wrap(x + dx, NX) * LANES, LANES), LANES)
-        return w_ref.at[panel, :, lanes]
 
     def w_go(here, there, where):
         dz, dyl, dx = there
@@ -320,12 +337,6 @@
         if here[:2] == (0, 0):
             w_go(here, (0, 1, dx), over_yl)
 
-    own_w = [
-        pltpu.make_async_copy(w_panel(0, panel), w_piece(0, 0, 0, panel), own_w_sem.at[panel])
-        for panel in range(3)
-    ]
-    for copy in own_w:
-        copy.start()
     for step in (1, 3, 2):
         for panel in range(3):
             go(
@@ -358,15 +369,17 @@
         if dx == 0:
             pass_on((3, dyh, 0, h), at_x(1))
             pass_on((1, dyh, 0, h), at_x(-1))
-        if (dx, dyh) == (0, 0):
-            pass_on((0, 1, 0, h), over_yh)
-        elif (dx, dyh) == (2, 0) and h % 2 == 1:
+        if (dx, dyh) == (2, 0) and h in (0, 1, 2, 3):
             pass_on((2, 1, 0, h), over_yh)
         elif dx in (1, 3):
-            turn = (3, 1, 3, 1) if dyh == 0 else (3, 0, 1, 0)
+            turn = (3, 1, 3, 1) if dyh == 0 else (0, 0, 0, 0)
             if turn[h] == dx:
                 pass_on((2, dyh, 0, h), at_x(1 if dx == 3 else -1))
         pass_on((dx, dyh, 1, h), over_core)
+
+    def features_over_yh(h):
+        src = feat_ref.at[pl.ds(h * FROWS, FROWS)]
+        go(f_started, f_send, src, f_piece(0, 0, 0, h), f_sem(0, 1, 0, h), over_yh)
 
     def filter_rows(part, ref, chunk):
         lanes = pl.ds(pl.multiple_of(chunk * LANES, LANES), LANES)
@@ -400,12 +413,42 @@
         h_copy(m, where).start()
         return carry
 
+    def project(dx, dzs, ends):
+        chunk = wrap(x + dx, NX)
+        if ends % 2:
+            if dx == 0:
+                own_f.wait()
+            for dyh in (0, 1):
+                for h in range(FPARTS):
+                    arrived(f_piece(dx, dyh, 1, h), f_sem(dx, dyh, 1, h))
+        total = None if ends % 2 else acc[dx]
+        for dz in dzs:
+            pz = wrap(z + dz, NZ)
+            lanes = pl.ds(pl.multiple_of(lax.rem(pz, 4) * WROWS, WROWS), WROWS)
+            for pyl in range(YL):
+                part = dot(feat[chunk, pyl * 2 + pz // 4, :, lanes], wbuf[pyl * NZ + pz])
+                total = part if total is None else total + part
+        if ends < 2:
+            acc[dx] = total
+            return
+        rounded = total.astype(BF16)
+        signal = rounded[:, :LANES].astype(F32) * rounded[:, LANES : 2 * LANES].astype(F32)
+        gmsg[chunk] = rounded[:, 2 * LANES :]
+        turned = signal.T
+        parts = [turned[:, i * N1 : (i + 1) * N1].reshape(Q, 1, CB, N1) for i in range(2)]
+        stacked = jnp.concatenate(parts, 1).reshape(Q, 2 * CB, N1)
+        sigmsg[:, pl.ds(pl.multiple_of(chunk * 16, 16), 16)] = stacked.astype(BF16)
+
     own_h = pltpu.make_async_copy(hmsg.at[me_m], hbuf.at[:, own_rows], local_sem.at[2])
     for kind, one, two, three in PLAN:
         if kind == "W":
             weights_arrived(one, two, three)
         elif kind == "F":
             features_arrived(one, two, three)
+        elif kind == "Y":
+            features_over_yh(one)
+        elif kind == "P":
+            project(one, two, three)
         elif kind == "h":
             for fetch in fetches[:3]:
                 fetch.wait()
@@ -414,26 +457,6 @@
         elif kind == "H":
             share = NS // two
             lax.fori_loop(max(1, one * share), (one + 1) * share, send_h, 0)
-    own_f.wait()
-    for dx in range(NX):
-        for dyh in (0, 1):
-            for h in range(FPARTS):
-                arrived(f_piece(dx, dyh, 1, h), f_sem(dx, dyh, 1, h))
-
-    def project(chunk, carry):
-        total = dot(feat[chunk, 0], wbuf[0:4].reshape(DBLK, COLS))
-        for j in range(1, 4):
-            total = total + dot(feat[chunk, j], wbuf[4 * j : 4 * j + 4].reshape(DBLK, COLS))
-        rounded = total.astype(BF16)
-        signal = rounded[:, :LANES].astype(F32) * rounded[:, LANES : 2 * LANES].astype(F32)
-        gmsg[chunk] = rounded[:, 2 * LANES :]
-        turned = signal.T
-        parts = [turned[:, i * N1 : (i + 1) * N1].reshape(Q, 1, CB, N1) for i in range(2)]
-        stacked = jnp.concatenate(parts, 1).reshape(Q, 2 * CB, N1)
-        sigmsg[:, pl.ds(pl.multiple_of(chunk * 16, 16), 16)] = stacked.astype(BF16)
-        return carry
-
-    lax.fori_loop(0, NX, project, 0)
 
     def s_copy(target, where):
         return pltpu.make_async_remote_copy(
@@ -550,6 +573,8 @@
     lax.fori_loop(1, NS, send_y, 0)
     own_y = pltpu.make_async_copy(ybf.at[own_rows], ybuf.at[me_m], local_sem.at[5])
     own_y.start()
+    for copy in w_started + f_started:
+        copy.wait_send()
     own_g.wait()
     for copy in gates:
         copy.wait()
@@ -564,9 +589,6 @@
             out_ref[i * N1 : (i + 1) * N1, chunk * LANES : (chunk + 1) * LANES] = (
                 gate * block
             ).astype(BF16)
-
-    for copy in w_started + f_started:
-        copy.wait_send()
 
 
 def shards(features, w_in, filter_real, filter_imag, skip_gain):
@@ -596,6 +618,7 @@
             pltpu.VMEM((N1 * CB, N1), F32),
             pltpu.VMEM((N1 * CB, N1), F32),
             pltpu.VMEM((N1 * CB, N1), F32),
+            pltpu.VMEM((NX, ROWS, COLS), F32),
             pltpu.VMEM((ROWS, width), F32),
             pltpu.VMEM((ROWS, width), F32),
             pltpu.VMEM((1, width), F32),

time: 77.7 us -> 74.8 us (0.963)
  Pallas kernels: 75.8 us -> 73 us
    pallas_call x1, Pallas kernels: 75.8 us -> 73 us  [shards(): pl.pallas_call(kernel, out_shape=jax.ShapeDtypeStruct((ROWS, width), BF16...]
where the time goes in v4:
time: 74.8 us; the launch traced here: 74.7 us
  Pallas kernels  73 us (98%)
  local copies, waits for them, and re-layouts  1.67 us (2%)
    pallas_call x1, Pallas kernels, shards(): pl.pallas_call(kernel, out_shape=jax.ShapeDtypeStruct((ROWS, width), BF16...  73 us
    unnamed x1, local copies, waits for them, and re-layouts  1.67 us

profile of v4, /device:TPU:8, one launch (start us, length us, event | category | flops | bytes accessed | tf_op | source)
XLA Modules:
  0.0 74.7 jit_solution(12879330585309631352)
XLA Ops:
  0.0 73.0 %shard_map.73 = bf16[256,512]{1,0:T(8,128)(2,1)} custom-call(bf16[256,1024]{1,0:T(8,128)(2,1)} %feat_ref.1, bf16[3,64,512]{2,1,0:T(8,128)(2,1)} %bitcast.2, f32[256,512]{1,0:T(8,128)} %fre_hbm.1, f32[256,512]{1,0:T(8,128)} %fim_hbm.1, f32[1,512]{1,0:T(1,128)} %bitcast.3, bf16[1536,256]{1,0:T(8,128)(2,1)} %constant.4.clone.dft_hbm, ...), custom_call_target="tpu_custom_call" | custom-call | tf_op jit(solution)/shard_map/pallas_call | solution.py:601
  73.0 1.7 %copy.9 = bf16[256,512]{1,0:T(8,128)(2,1)} copy(bf16[256,512]{1,0:T(8,128)(2,1)} %shard_map.73) | data formatting | bytes 524288

commit v5 on v4

--- a/solution.py
+++ b/solution.py
@@ -26,6 +26,9 @@
 N1 = 128
 WROWS = 64 * NX
 COLS = 3 * LANES
+FAR_OVER_Y = (0, 1, 2, 3)
+FAR_TURN = (0, 0, 0, 0)
+OVER_Y = (0,)
 
 
 PLAN = (
@@ -36,6 +39,7 @@
     ("F", 0, 0, 2),
     ("F", 0, 0, 3),
     ("Y", 1, 0, 0),
+    ("h", 0, 0, 0),
     ("W", 0, 0, 1),
     ("W", 0, 0, 3),
     ("W", -1, 0, 0),
@@ -44,7 +48,6 @@
     ("W", 0, 1, 0),
     ("Y", 2, 0, 0),
     ("F", 1, 0, 0),
-    ("h", 0, 0, 0),
     ("W", -1, 0, 1),
     ("W", 1, 0, 1),
     ("F", 3, 0, 0),
@@ -122,21 +125,21 @@
     ("W", 3, 1, 3),
     ("W", -4, 0, 2),
     ("W", 3, 1, 2),
+    ("H", 0, 1, 0),
     ("F", 2, 1, 3),
     ("F", 1, 1, 3),
     ("W", -3, 1, 1),
     ("W", -4, 1, 1),
     ("F", 3, 1, 3),
-    ("H", 0, 1, 0),
     ("W", -3, 1, 3),
     ("W", -4, 1, 3),
     ("W", -3, 1, 2),
     ("F", 2, 1, 2),
     ("W", -4, 1, 2),
     ("P", 0, (-3, 3, -4), 2),
-    ("P", 1, (0, -1, 1, -2, 2, -3, 3, -4), 3),
-    ("P", 3, (0, -1, 1, -2, 2, -3, 3, -4), 3),
-    ("P", 2, (0, -1, 1, -2, 2, -3, 3, -4), 3),
+    ("P", 1, (-2, 2, 0, -1, 1, -3, 3, -4), 3),
+    ("P", 3, (-3, 3, -2, 2, 0, -1, 1, -4), 3),
+    ("P", 2, (-4, -3, 3, -2, 2, 0, -1, 1), 3),
 )
 
 
@@ -173,11 +176,10 @@
     return lax.dot_general(a, b, (((1,), (1,)), ((), ())), preferred_element_type=F32)
 
 
-def three_pass(product, stacked, value):
+def two_pass(product, stacked, value):
     m = stacked.shape[0] // 2
-    high, low = split16(value)
-    both = product(stacked, high)
-    return both[:m] + both[m:] + product(stacked[:m], low)
+    both = product(stacked, value.astype(BF16))
+    return both[:m] + both[m:]
 
 
 def kernel(
@@ -284,7 +286,7 @@
 
     barrier = pltpu.get_barrier_semaphore()
 
-    for where in (at_x(1),at_x(2),at_x(-1),at_z(1),at_z(-1),over_yl):
+    for where in (at_x(1), at_x(2), at_x(-1), at_z(1), at_z(-1), over_yl):
         pl.semaphore_signal(barrier, inc=1, device_id=where, device_id_type=MESH)
     pl.semaphore_signal(barrier, inc=1, device_id=over_yh, device_id_type=MESH)
     pl.semaphore_signal(barrier, inc=1, device_id=over_core, device_id_type=MESH)
@@ -330,12 +332,13 @@
                 arrived(w_piece(0, 0, dx, panel), ws_recv.at[(dx - 1) * 3 + panel])
         else:
             arrived(w_piece(*here), w_recv.at[(dz % NZ * 2 + dyl) * NX + dx])
-        if -3 < dz <= 0 or (dz == -3 and dyl == 0):
+        left, right = (dz - 1) % NZ, (dz + 1) % NZ
+        if (-3 < dz <= 0 or (dz == -3 and dyl == 0)) and not (dyl == 1 and left in OVER_Y):
             w_go(here, (dz - 1, dyl, dx), at_z(1))
-        if 0 <= dz < 3 or (dz == 3 and dyl == 1):
+        if (0 <= dz < 3 or (dz == 3 and dyl == 1)) and not (dyl == 1 and right in OVER_Y):
             w_go(here, (dz + 1, dyl, dx), at_z(-1))
-        if here[:2] == (0, 0):
-            w_go(here, (0, 1, dx), over_yl)
+        if dyl == 0 and dz % NZ in OVER_Y:
+            w_go(here, (dz, 1, dx), over_yl)
 
     for step in (1, 3, 2):
         for panel in range(3):
@@ -369,10 +372,10 @@
         if dx == 0:
             pass_on((3, dyh, 0, h), at_x(1))
             pass_on((1, dyh, 0, h), at_x(-1))
-        if (dx, dyh) == (2, 0) and h in (0, 1, 2, 3):
+        if (dx, dyh) == (2, 0) and h in FAR_OVER_Y:
             pass_on((2, 1, 0, h), over_yh)
         elif dx in (1, 3):
-            turn = (3, 1, 3, 1) if dyh == 0 else (0, 0, 0, 0)
+            turn = (3, 1, 3, 1) if dyh == 0 else FAR_TURN
             if turn[h] == dx:
                 pass_on((2, dyh, 0, h), at_x(1 if dx == 3 else -1))
         pass_on((dx, dyh, 1, h), over_core)
@@ -543,14 +546,14 @@
         step1 = dot(first, jnp.concatenate([value, value], 0))
         re, im = step1[:N1], step1[N1:]
         turned = stack(re * tc + im * ts, im * tc - re * ts)
-        spectrum = three_pass(dot_nt, forward, turned)
+        spectrum = two_pass(dot_nt, forward, turned)
         re, im = spectrum[:N1], spectrum[N1:]
         fr, fi = lanes(hre), lanes(him)
         filtered = jnp.concatenate([fr * re - fi * im, fr * im + fi * re], 0)
-        step3 = three_pass(dot, back, filtered)
+        step3 = two_pass(dot, back, filtered)
         re, im = step3[:N1], step3[N1:]
         turned = stack(re * tc - im * ts, im * tc + re * ts)
-        result = three_pass(dot_nt, last, turned)
+        result = two_pass(dot_nt, last, turned)
         for g in range(GROUP):
             yf[rows[g], :] = result[:, g * N1 : (g + 1) * N1]
     ybf[...] = yf[...].astype(BF16)
@@ -626,7 +629,7 @@
             pltpu.VMEM((2, N1, N1), F32),
             dma((80,)),
             dma((16 * FPARTS,)),
-            dma((80,)),
+            dma((100,)),
             dma((9,)),
             dma((64,)),
             dma((3,)),

time: 74.8 us -> 74.1 us (level)
  no operation moved by 1% of the time
where the time goes in v5:
time: 74.1 us; the launch traced here: 74 us
  Pallas kernels  72.3 us (98%)
  local copies, waits for them, and re-layouts  1.67 us (2%)
    pallas_call x1, Pallas kernels, shards(): pl.pallas_call(kernel, out_shape=jax.ShapeDtypeStruct((ROWS, width), BF16...  72.3 us
    unnamed x1, local copies, waits for them, and re-layouts  1.67 us

profile of v5, /device:TPU:8, one launch (start us, length us, event | category | flops | bytes accessed | tf_op | source)
XLA Modules:
  0.0 74.0 jit_solution(8798894885953129136)
XLA Ops:
  0.0 72.3 %shard_map.73 = bf16[256,512]{1,0:T(8,128)(2,1)} custom-call(bf16[256,1024]{1,0:T(8,128)(2,1)} %feat_ref.1, bf16[3,64,512]{2,1,0:T(8,128)(2,1)} %bitcast.2, f32[256,512]{1,0:T(8,128)} %fre_hbm.1, f32[256,512]{1,0:T(8,128)} %fim_hbm.1, f32[1,512]{1,0:T(1,128)} %bitcast.3, bf16[1536,256]{1,0:T(8,128)(2,1)} %constant.4.clone.dft_hbm, ...), custom_call_target="tpu_custom_call" | custom-call | tf_op jit(solution)/shard_map/pallas_call | solution.py:604
  72.4 1.7 %copy.9 = bf16[256,512]{1,0:T(8,128)(2,1)} copy(bf16[256,512]{1,0:T(8,128)(2,1)} %shard_map.73) | data formatting | bytes 524288
